TPU v7x, 256 devices: a whole 4x4x8 slice. The times are simulated.
256 devices in a mesh: row: 16 (over x, y), col: 16 (over z, core).
Axes of the slice: x: 4, y: 4, z: 8, core: 2. Of those that a mesh axis runs over, the one named last changes fastest.
Arguments:
- activations: bfloat16 [8192, 2048], P('row'), may hold values from -6 to 6
- cotangent: bfloat16 [8192, 2048], P('row'), may hold values from -6 to 6
- router: float32 [2048, 16], replicated, may hold values from -3 to 3
- gate_experts: bfloat16 [16, 2048, 5632], P(None, 'row', 'col'), may hold values from -0.125 to 0.125
- up_experts: bfloat16 [16, 2048, 5632], P(None, 'row', 'col'), may hold values from -0.125 to 0.125
- down_experts: bfloat16 [16, 5632, 2048], P(None, 'col', 'row'), may hold values from -0.078125 to 0.078125
- route_source: int32 [32], replicated, may hold values from 0 to 30, as said below
Outputs:
- input_grad: bfloat16 [8192, 2048], P('row')
- gate_grad: bfloat16 [16, 2048, 5632], P(None, 'row', 'col')
- up_grad: bfloat16 [16, 2048, 5632], P(None, 'row', 'col')
- down_grad: bfloat16 [16, 5632, 2048], P(None, 'col', 'row')
- router_grad: float32 [2048, 16], replicated
Inputs may be any that keep to these rules, and one draw needn't show every extreme that they name: route_source[0] = 0, and for every later segment s it names s - 1 or s - 2 (never below 0); the last segment names 30.
All inputs are finite; a program needn't handle non-finite values.
Results may differ from a plain program's by a relative error of at most 0.011.
Values may be sent and summed in bfloat16 or wider, within the bound.
A program may use at most 128 MiB of HBM per device.

v0:
```python
import jax
import jax.numpy as jnp
from jax import lax
from jax.sharding import PartitionSpec as P

SEG_LEN = 256


PRECISE = lax.Precision.HIGHEST


def shards(activations, cotangent, router, gate_experts, up_experts, down_experts, route_source):
    model_width = activations.shape[1]
    segs_here = activations.shape[0] // SEG_LEN
    seg_count = segs_here * lax.axis_size("row")
    first_seg = lax.axis_index("row") * segs_here
    block_list = activations.reshape(segs_here, SEG_LEN, model_width)
    output_gradients = cotangent.reshape(segs_here, SEG_LEN, model_width)
    own_means = jnp.mean(block_list, axis=1, dtype=jnp.float32)
    all_means = lax.all_gather(own_means, "row", axis=0, tiled=True)
    all_scores = jnp.dot(all_means, router, precision=PRECISE)
    chooser = (route_source[:, None] == jnp.arange(seg_count, dtype=jnp.int32)[None, :]).astype(
        jnp.float32
    )
    logits = jnp.dot(chooser, all_scores, precision=PRECISE)
    powers = jnp.exp(logits)
    routes = powers / jnp.sum(powers, axis=-1, keepdims=True)
    rounded = routes.astype(jnp.bfloat16)
    local_gate = jnp.einsum(
        "se,edf->sdf", rounded, gate_experts, preferred_element_type=jnp.float32
    ).astype(jnp.bfloat16)
    local_up = jnp.einsum(
        "se,edf->sdf", rounded, up_experts, preferred_element_type=jnp.float32
    ).astype(jnp.bfloat16)
    local_down = jnp.einsum(
        "se,efd->sdf", rounded, down_experts, preferred_element_type=jnp.float32
    ).astype(jnp.bfloat16)
    combined_gate_weight, combined_up_weight, combined_down_weight = (
        lax.all_to_all(local_gate, "row", split_axis=0, concat_axis=1, tiled=True),
        lax.all_to_all(local_up, "row", split_axis=0, concat_axis=1, tiled=True),
        lax.all_to_all(local_down, "row", split_axis=0, concat_axis=1, tiled=True),
    )
    gate_preactivation = jnp.einsum(
        "wzp,wpg->wzg", block_list, combined_gate_weight, preferred_element_type=jnp.float32
    )
    up_preactivation = jnp.einsum(
        "wzp,wpg->wzg", block_list, combined_up_weight, preferred_element_type=jnp.float32
    )
    sigmoid_gate = jax.nn.sigmoid(gate_preactivation)
    gate_act = gate_preactivation * sigmoid_gate
    hidden_state = (gate_act * up_preactivation).astype(jnp.bfloat16)
    hidden_grad = jnp.einsum(
        "wzp,wpg->wzg", output_gradients, combined_down_weight, preferred_element_type=jnp.float32
    )
    gate_difference = (
        hidden_grad
        * up_preactivation
        * sigmoid_gate
        * (1.0 + gate_preactivation * (1.0 - sigmoid_gate))
    ).astype(jnp.bfloat16)
    up_difference = (hidden_grad * gate_act).astype(jnp.bfloat16)
    direct_local = jnp.einsum(
        "kri,kvi->krv", gate_difference, combined_gate_weight, preferred_element_type=jnp.float32
    )
    direct_local = direct_local + jnp.einsum(
        "kri,kvi->krv", up_difference, combined_up_weight, preferred_element_type=jnp.float32
    )
    direct_grad = lax.psum(direct_local, "col")
    gate_own = jnp.einsum(
        "wgt,wgn->wtn", block_list, gate_difference, preferred_element_type=jnp.float32
    ).astype(jnp.bfloat16)
    up_own = jnp.einsum(
        "wgt,wgn->wtn", block_list, up_difference, preferred_element_type=jnp.float32
    ).astype(jnp.bfloat16)
    down_own = jnp.einsum(
        "wgt,wgn->wtn", output_gradients, hidden_state, preferred_element_type=jnp.float32
    ).astype(jnp.bfloat16)
    gate_terms, up_terms, down_terms = (
        lax.all_to_all(gate_own, "row", split_axis=1, concat_axis=0, tiled=True),
        lax.all_to_all(up_own, "row", split_axis=1, concat_axis=0, tiled=True),
        lax.all_to_all(down_own, "row", split_axis=1, concat_axis=0, tiled=True),
    )
    partial_value = jnp.einsum(
        "edf,sdf->se", gate_experts, gate_terms, preferred_element_type=jnp.float32
    )
    partial_value = partial_value + jnp.einsum(
        "edf,sdf->se", up_experts, up_terms, preferred_element_type=jnp.float32
    )
    partial_value = partial_value + jnp.einsum(
        "efd,sdf->se", down_experts, down_terms, preferred_element_type=jnp.float32
    )
    route_grad = lax.psum(partial_value, ("row", "col"))
    logit_grad = routes * (route_grad - jnp.sum(routes * route_grad, axis=-1, keepdims=True))
    source_grad = jnp.dot(chooser.T, logit_grad, precision=PRECISE)
    own_source = lax.dynamic_slice_in_dim(source_grad, first_seg, segs_here, 0)
    router_grad = jnp.dot(all_means.T, source_grad, precision=PRECISE)
    mean_grad = jnp.dot(own_source, router.T, precision=PRECISE)
    input_grad = (
        (direct_grad + mean_grad[:, None, :] / SEG_LEN)
        .reshape(-1, model_width)
        .astype(jnp.bfloat16)
    )
    gate_grad = jnp.einsum(
        "se,sdf->edf", rounded, gate_terms, preferred_element_type=jnp.float32
    ).astype(jnp.bfloat16)
    up_grad = jnp.einsum(
        "se,sdf->edf", rounded, up_terms, preferred_element_type=jnp.float32
    ).astype(jnp.bfloat16)
    down_grad = jnp.einsum(
        "se,sdf->efd", rounded, down_terms, preferred_element_type=jnp.float32
    ).astype(jnp.bfloat16)
    return (input_grad, gate_grad, up_grad, down_grad, router_grad)


def solution(mesh):
    in_specs = (
        P("row", None),
        P("row", None),
        P(),
        P(None, "row", "col"),
        P(None, "row", "col"),
        P(None, "col", "row"),
        P(),
    )
    out_specs = (
        P("row", None),
        P(None, "row", "col"),
        P(None, "row", "col"),
        P(None, "col", "row"),
        P(),
    )
    return jax.shard_map(shards, mesh=mesh, in_specs=in_specs, out_specs=out_specs, check_vma=False)
```

profile of v0, /device:TPU:1, one launch (start us, length us, event | category | flops | bytes accessed | tf_op | source)
XLA Modules:
  0.0 409.3 jit_solution(5258795962054658265)
XLA Ops:
  9.4 21.6 %all-gather = f32[16,2,2048]{2,1,0:T(2,128)} all-gather(f32[1,2,2048]{2,1,0:T(2,128)S(1)} %multiply_bitcast_fusion), channel_id=1, replica_groups=mesh['row'=16,'col'=16] {'row'}, dimensions={0}, use_global_device_ids=true | all-gather | bytes 278528 | tf_op jit(solution)/shard_map/all_gather | solution.py:20
  35.3 2.7 copy.31
  38.0 4.6 %all-to-all-start.1 = ((bf16[32,128,352]{1,2,0:T(8,128)(2,1)}), bf16[32,128,352]{1,2,0:T(8,128)(2,1)}, u32[]{:S(2)}, u32[]{:S(2)}) async-start(bf16[32,128,352]{1,2,0:T(8,128)(2,1)} %copy.31), calls=%async_computation.1 | async-start | bytes 5767168 | tf_op jit(solution)/shard_map/all_to_all | solution.py:40
  46.3 27.3 %all-to-all-done.1 = bf16[32,128,352]{1,2,0:T(8,128)(2,1)} async-done(((bf16[32,128,352]{1,2,0:T(8,128)(2,1)}), bf16[32,128,352]{1,2,0:T(8,128)(2,1)}, u32[]{:S(2)}, u32[]{:S(2)}) %all-to-all-start.1) | async-done | bytes 2883616 | tf_op jit(solution)/shard_map/all_to_all | solution.py:40
  73.6 8.6 %all-to-all-start.2 = ((bf16[32,128,352]{1,2,0:T(8,128)(2,1)}), bf16[32,128,352]{1,2,0:T(8,128)(2,1)}, u32[]{:S(2)}, u32[]{:S(2)}) async-start(bf16[32,128,352]{1,2,0:T(8,128)(2,1)} %copy.34), calls=%async_computation.2 | async-start | bytes 5767168 | tf_op jit(solution)/shard_map/all_to_all | solution.py:39
  83.2 2.8 copy.28
  85.9 28.1 %all-to-all-done.2 = bf16[32,128,352]{1,2,0:T(8,128)(2,1)} async-done(((bf16[32,128,352]{1,2,0:T(8,128)(2,1)}), bf16[32,128,352]{1,2,0:T(8,128)(2,1)}, u32[]{:S(2)}, u32[]{:S(2)}) %all-to-all-start.2) | async-done | bytes 2883616 | tf_op jit(solution)/shard_map/all_to_all | solution.py:39
  114.1 7.8 %all-to-all-start = ((bf16[32,128,352]{1,2,0:T(8,128)(2,1)}), bf16[32,128,352]{1,2,0:T(8,128)(2,1)}, u32[]{:S(2)}, u32[]{:S(2)}) async-start(bf16[32,128,352]{1,2,0:T(8,128)(2,1)} %copy.28), calls=%async_computation | async-start | bytes 5767168 | tf_op jit(solution)/shard_map/all_to_all | solution.py:41
  121.8 5.3 %copy.74 = bf16[16,2,128,352]{2,0,3,1:T(8,128)(2,1)} copy(bf16[16,2,128,352]{2,3,1,0:T(8,128)(2,1)} %bitcast.8) | data formatting | bytes 5767168 | tf_op jit(solution)/shard_map/all_to_all | solution.py:40
  127.1 5.6 %all_to_all.85 = bf16[2,2048,352]{1,2,0:T(8,128)(2,1)} reshape(bf16[2,16,128,352]{2,1,3,0:T(8,128)(2,1)} %bitcast.120) | data formatting | bytes 5767168 | tf_op jit(solution)/shard_map/all_to_all | solution.py:40
  132.7 5.3 %copy.73 = bf16[16,2,128,352]{2,0,3,1:T(8,128)(2,1)} copy(bf16[16,2,128,352]{2,3,1,0:T(8,128)(2,1)} %bitcast.11) | data formatting | bytes 5767168 | tf_op jit(solution)/shard_map/all_to_all | solution.py:39
  137.9 5.5 %all_to_all.89 = bf16[2,2048,352]{1,2,0:T(8,128)(2,1)} reshape(bf16[2,16,128,352]{2,1,3,0:T(8,128)(2,1)} %bitcast.121) | data formatting | bytes 5767168 | tf_op jit(solution)/shard_map/all_to_all | solution.py:39
  143.5 3.5 convolution_bitcast_fusion.1
  151.8 8.7 %copy.42 = bf16[2,2048,352]{2,0,1:T(2,128)(2,1)} copy(bf16[2,2048,352]{1,2,0:T(8,128)(2,1)} %fusion.2) | data formatting | bytes 5767168 | tf_op jit(solution)/shard_map/convert_element_type | solution.py:77
  160.5 6.7 %all-to-all-start.5 = ((bf16[2,2048,352]{2,0,1:T(2,128)(2,1)}), bf16[2,2048,352]{2,0,1:T(2,128)(2,1)}, u32[]{:S(2)}, u32[]{:S(2)}) async-start(bf16[2,2048,352]{2,0,1:T(2,128)(2,1)} %copy.42), calls=%async_computation.5 | async-start | bytes 6291456 | tf_op jit(solution)/shard_map/all_to_all | solution.py:81
  167.2 5.2 %copy.75 = bf16[16,2,128,352]{2,0,3,1:T(8,128)(2,1)} copy(bf16[16,2,128,352]{2,3,1,0:T(8,128)(2,1)} %bitcast.4) | data formatting | bytes 5767168 | tf_op jit(solution)/shard_map/all_to_all | solution.py:41
  172.4 5.6 %all_to_all.81 = bf16[2,2048,352]{1,2,0:T(8,128)(2,1)} reshape(bf16[2,16,128,352]{2,1,3,0:T(8,128)(2,1)} %bitcast.122) | data formatting | bytes 5767168 | tf_op jit(solution)/shard_map/all_to_all | solution.py:41
  178.0 4.2 %multiply_convert_fusion.1 = (bf16[2,256,352]{1,2,0:T(8,128)(2,1)S(1)}, bf16[2,256,352]{1,2,0:T(8,128)(2,1)}) fusion(f32[2,256,352]{1,2,0:T(8,128)} %copy-done.16, f32[2,256,352]{1,2,0:T(8,128)} %copy-done.15, bf16[2,2048,352]{1,2,0:T(8,128)(2,1)} %all_to_all.81, bf16[2,256,2048]{2,1,0:T(8,128)(2,1)S(1)} %bitcast.108), kind=kOutput, calls=%fused_computation.39 | convolution fusion | flops 740540416 | bytes 7143424 | tf_op jit(solution)/shard_map/wzp,wpg->wzg/dot_general | solution.py:52
  185.4 8.7 %copy.39 = bf16[2,2048,352]{2,0,1:T(2,128)(2,1)} copy(bf16[2,2048,352]{1,2,0:T(8,128)(2,1)} %fusion.1) | data formatting | bytes 5767168 | tf_op jit(solution)/shard_map/convert_element_type | solution.py:74
  194.1 5.9 %all-to-all-done.5 = bf16[2,2048,352]{2,0,1:T(2,128)(2,1)} async-done(((bf16[2,2048,352]{2,0,1:T(2,128)(2,1)}), bf16[2,2048,352]{2,0,1:T(2,128)(2,1)}, u32[]{:S(2)}, u32[]{:S(2)}) %all-to-all-start.5) | async-done | bytes 2883616 | tf_op jit(solution)/shard_map/all_to_all | solution.py:81
  200.0 10.8 %all-to-all-start.4 = ((bf16[2,2048,352]{2,0,1:T(2,128)(2,1)}), bf16[2,2048,352]{2,0,1:T(2,128)(2,1)}, u32[]{:S(2)}, u32[]{:S(2)}) async-start(bf16[2,2048,352]{2,0,1:T(2,128)(2,1)} %copy.39), calls=%async_computation.4 | async-start | bytes 6291456 | tf_op jit(solution)/shard_map/all_to_all | solution.py:80
  210.9 3.5 fusion
  214.4 8.7 %copy.36 = bf16[2,2048,352]{2,0,1:T(2,128)(2,1)} copy(bf16[2,2048,352]{1,2,0:T(8,128)(2,1)} %fusion) | data formatting | bytes 5767168 | tf_op jit(solution)/shard_map/convert_element_type | solution.py:71
  223.1 23.9 %all-to-all-done.4 = bf16[2,2048,352]{2,0,1:T(2,128)(2,1)} async-done(((bf16[2,2048,352]{2,0,1:T(2,128)(2,1)}), bf16[2,2048,352]{2,0,1:T(2,128)(2,1)}, u32[]{:S(2)}, u32[]{:S(2)}) %all-to-all-start.4) | async-done | bytes 2883616 | tf_op jit(solution)/shard_map/all_to_all | solution.py:80
  246.9 9.8 %all-to-all-start.3 = ((bf16[2,2048,352]{2,0,1:T(2,128)(2,1)}), bf16[2,2048,352]{2,0,1:T(2,128)(2,1)}, u32[]{:S(2)}, u32[]{:S(2)}) async-start(bf16[2,2048,352]{2,0,1:T(2,128)(2,1)} %copy.36), calls=%async_computation.3 | async-start | bytes 6291456 | tf_op jit(solution)/shard_map/all_to_all | solution.py:79
  257.1 3.3 fusion.48
  260.4 3.3 convolution_add_fusion
  263.7 11.2 %copy.43 = bf16[2,16,128,352]{2,0,1,3:T(2,128)(2,1)} copy(bf16[2,16,128,352]{3,0,2,1:T(2,128)(2,1)} %bitcast.25) | data formatting | bytes 5767168 | tf_op jit(solution)/shard_map/all_to_all | solution.py:81
  278.7 11.2 %copy.40 = bf16[2,16,128,352]{2,0,1,3:T(2,128)(2,1)} copy(bf16[2,16,128,352]{3,0,2,1:T(2,128)(2,1)} %bitcast.20) | data formatting | bytes 5767168 | tf_op jit(solution)/shard_map/all_to_all | solution.py:80
  293.7 11.2 %copy.37 = bf16[2,16,128,352]{2,0,1,3:T(2,128)(2,1)} copy(bf16[2,16,128,352]{3,0,2,1:T(2,128)(2,1)} %bitcast.15) | data formatting | bytes 5767168 | tf_op jit(solution)/shard_map/all_to_all | solution.py:79
  314.4 82.6 %psum.15 = f32[32,16]{0,1:T(8,128)S(1)} all-reduce(f32[32,16]{0,1:T(8,128)S(1)} %fusion.25), channel_id=1, replica_groups=mesh['row'=16,'col'=16] {'row','col'}, use_global_device_ids=true, to_apply=%region_3.0 | all-reduce | flops 512 | bytes 4096 | tf_op jit(solution)/shard_map/psum | solution.py:92
  398.5 4.0 add_convert_fusion
  (79 shorter events, 37.8 us)
Async XLA Ops:
  7.2 141.2 %copy-start = (bf16[512,2048]{1,0:T(8,128)(2,1)S(1)}, bf16[512,2048]{1,0:T(8,128)(2,1)}, u32[]{:S(2)}) copy-start(bf16[512,2048]{1,0:T(8,128)(2,1)} %param.8) | copy-start | bytes 6291460
  7.2 26.9 %copy-start.22 = (s32[32]{0:T(128)S(1)}, s32[32]{0:T(128)}, u32[]{:S(2)}) copy-start(s32[32]{0:T(128)} %param.13) | copy-start | bytes 388
  7.2 27.2 %copy-start.11 = (bf16[16,128,352]{1,2,0:T(8,128)(2,1)S(1)}, bf16[16,128,352]{1,2,0:T(8,128)(2,1)}, u32[]{:S(2)}) copy-start(bf16[16,128,352]{1,2,0:T(8,128)(2,1)} %param.11) | copy-start | bytes 4325380
  38.0 4.6 %copy-start.13 = (bf16[16,128,352]{1,2,0:T(8,128)(2,1)S(1)}, bf16[16,128,352]{1,2,0:T(8,128)(2,1)}, u32[]{:S(2)}) copy-start(bf16[16,128,352]{1,2,0:T(8,128)(2,1)} %param.10) | copy-start | bytes 4325380
  38.0 35.6 %all-to-all-start.1 = ((bf16[32,128,352]{1,2,0:T(8,128)(2,1)}), bf16[32,128,352]{1,2,0:T(8,128)(2,1)}, u32[]{:S(2)}, u32[]{:S(2)}) async-start(bf16[32,128,352]{1,2,0:T(8,128)(2,1)} %copy.31), calls=%async_computation.1 | async-start | bytes 5767168 | tf_op jit(solution)/shard_map/all_to_all | solution.py:40
  46.3 35.9 %copy-start.10 = (bf16[16,352,128]{2,1,0:T(8,128)(2,1)S(1)}, bf16[16,352,128]{2,1,0:T(8,128)(2,1)}, u32[]{:S(2)}) copy-start(bf16[16,352,128]{2,1,0:T(8,128)(2,1)} %param.12) | copy-start | bytes 4325380
  73.6 40.5 %all-to-all-start.2 = ((bf16[32,128,352]{1,2,0:T(8,128)(2,1)}), bf16[32,128,352]{1,2,0:T(8,128)(2,1)}, u32[]{:S(2)}, u32[]{:S(2)}) async-start(bf16[32,128,352]{1,2,0:T(8,128)(2,1)} %copy.34), calls=%async_computation.2 | async-start | bytes 5767168 | tf_op jit(solution)/shard_map/all_to_all | solution.py:39
  114.1 46.4 %all-to-all-start = ((bf16[32,128,352]{1,2,0:T(8,128)(2,1)}), bf16[32,128,352]{1,2,0:T(8,128)(2,1)}, u32[]{:S(2)}, u32[]{:S(2)}) async-start(bf16[32,128,352]{1,2,0:T(8,128)(2,1)} %copy.28), calls=%async_computation | async-start | bytes 5767168 | tf_op jit(solution)/shard_map/all_to_all | solution.py:41
  143.5 3.6 copy-start.2
  143.5 3.9 copy-start.5
  147.4 1.0 copy-start.15
  148.4 0.9 copy-start.16
  160.5 39.5 %all-to-all-start.5 = ((bf16[2,2048,352]{2,0,1:T(2,128)(2,1)}), bf16[2,2048,352]{2,0,1:T(2,128)(2,1)}, u32[]{:S(2)}, u32[]{:S(2)}) async-start(bf16[2,2048,352]{2,0,1:T(2,128)(2,1)} %copy.42), calls=%async_computation.5 | async-start | bytes 6291456 | tf_op jit(solution)/shard_map/all_to_all | solution.py:81
  178.0 4.9 %copy-start.3 = (bf16[512,2048]{1,0:T(8,128)(2,1)S(1)}, bf16[512,2048]{1,0:T(8,128)(2,1)}, u32[]{:S(2)}) copy-start(bf16[512,2048]{1,0:T(8,128)(2,1)} %param.7) | copy-start | bytes 6291460
  182.2 0.7 copy-start.18
  194.1 16.7 %copy-start.4 = (bf16[512,2048]{1,0:T(8,128)(2,1)S(1)}, bf16[512,2048]{1,0:T(8,128)(2,1)}, u32[]{:S(2)}) copy-start(bf16[512,2048]{1,0:T(8,128)(2,1)} %param.7) | copy-start | bytes 6291460
  200.0 46.9 %all-to-all-start.4 = ((bf16[2,2048,352]{2,0,1:T(2,128)(2,1)}), bf16[2,2048,352]{2,0,1:T(2,128)(2,1)}, u32[]{:S(2)}, u32[]{:S(2)}) async-start(bf16[2,2048,352]{2,0,1:T(2,128)(2,1)} %copy.39), calls=%async_computation.4 | async-start | bytes 6291456 | tf_op jit(solution)/shard_map/all_to_all | solution.py:80
  223.1 34.0 %copy-start.20 = (bf16[2,256,352]{1,2,0:T(8,128)(2,1)S(1)}, bf16[2,256,352]{1,2,0:T(8,128)(2,1)}, u32[]{:S(2)}) copy-start(bf16[2,256,352]{1,2,0:T(8,128)(2,1)} %get-tuple-element.16) | copy-start | bytes 1081348
  246.9 46.8 %all-to-all-start.3 = ((bf16[2,2048,352]{2,0,1:T(2,128)(2,1)}), bf16[2,2048,352]{2,0,1:T(2,128)(2,1)}, u32[]{:S(2)}, u32[]{:S(2)}) async-start(bf16[2,2048,352]{2,0,1:T(2,128)(2,1)} %copy.36), calls=%async_computation.3 | async-start | bytes 6291456 | tf_op jit(solution)/shard_map/all_to_all | solution.py:79
  256.8 141.7 %all-reduce.2.cloned.1.call-start = ((), (), s32[]{:S(2)}) async-start(), calls=%async_computation.6 | async-start | bytes 8388608 | tf_op jit(solution)/shard_map/psum | solution.py:68
  257.1 3.3 copy-start.6
  257.1 3.3 copy-start.19
  304.9 4.0 copy-start.7
  309.0 1.8 copy-start.8
  309.0 2.2 copy-start.12
  311.2 1.8 copy-start.9
  311.2 2.3 copy-start.14
  313.5 83.5 %copy-start.23 = (s32[32]{0:T(128)S(1)}, s32[32]{0:T(128)}, u32[]{:S(2)}) copy-start(s32[32]{0:T(128)} %param.13) | copy-start | bytes 388
  313.5 83.7 %copy-start.21 = (f32[2048,16]{0,1:T(8,128)S(1)}, f32[2048,16]{0,1:T(8,128)}, u32[]{:S(2)}) copy-start(f32[2048,16]{0,1:T(8,128)} %param.9) | copy-start | bytes 393220
  313.5 84.0 %copy-start.17 = (f32[32,2048]{1,0:T(8,128)S(1)}, f32[32,2048]{1,0:T(8,128)}, u32[]{:S(2)}) copy-start(f32[32,2048]{1,0:T(8,128)} %reshape.26) | copy-start | bytes 786436
  397.5 5.0 %copy-start.1 = (bf16[512,2048]{1,0:T(8,128)(2,1)S(1)}, bf16[512,2048]{1,0:T(8,128)(2,1)}, u32[]{:S(2)}) copy-start(bf16[512,2048]{1,0:T(8,128)(2,1)} %param.8) | copy-start | bytes 6291460
Sparse Core Ops, SparseCore 0:
  263.8 125.7 all-reduce.1
where the time goes:
time: 412 us; the launch traced here: 409 us
  local copies, waits for them, and re-layouts  111 us (27%)
  blocking collectives  104 us (25%)
  waiting for transfers between devices  85.3 us (21%)
  starting transfers between devices  48.6 us (12%)
  matrix products  39.6 us (10%)
  between operations  14.4 us (3%)
  other arithmetic  6.18 us (2%)
    psum x1, blocking collectives, shards(): route_grad = lax.psum(partial_value, ('row', 'col'))  82.6 us
    all_to_all x1, waiting for transfers between devices, shards(): lax.all_to_all(local_gate, 'row', split_axis=0, concat_axis=1, tiled=True)  28.1 us
    all_to_all x1, waiting for transfers between devices, shards(): lax.all_to_all(local_up, 'row', split_axis=0, concat_axis=1, tiled=True)  27.3 us
    all_to_all x1, waiting for transfers between devices, shards(): lax.all_to_all(up_own, 'row', split_axis=1, concat_axis=0, tiled=True)  23.9 us
    all_gather x1, blocking collectives, shards(): all_means = lax.all_gather(own_means, 'row', axis=0, tiled=True)  21.6 us
    all_to_all x1, local copies, waits for them, and re-layouts, shards(): lax.all_to_all(up_own, 'row', split_axis=1, concat_axis=0, tiled=True)  11.2 us
    all_to_all x1, local copies, waits for them, and re-layouts, shards(): lax.all_to_all(gate_own, 'row', split_axis=1, concat_axis=0, tiled=True)  11.2 us
    all_to_all x1, local copies, waits for them, and re-layouts, shards(): lax.all_to_all(down_own, 'row', split_axis=1, concat_axis=0, tiled=True)  11.2 us
  transfers between devices with their start and end apart: 7, of which 4 were waited for; matrix products, arithmetic and copies ran while one was open for 30% of the time, Pallas kernels for 0%

commit v1 on v0

v1 whole, which is shorter than its diff:
```python
import functools

import jax
import jax.numpy as jnp
from jax import lax
from jax.experimental import pallas as pl
from jax.experimental.pallas import tpu as pltpu
from jax.sharding import PartitionSpec as P

SEG = 256
EXPERTS = 16
SIDE = 4
DEPTH = 8
BLOCK = 128
HALF = 176
LANES = 3 * BLOCK
WIDE = SIDE * BLOCK
GROUP = 16
CHUNK = 16
PRECISE = lax.Precision.HIGHEST
MESH = pl.DeviceIdType.MESH
F32 = jnp.float32
BF16 = jnp.bfloat16


def dot_nn(a, b):
    return lax.dot_general(a, b, (((1,), (0,)), ((), ())), preferred_element_type=F32)


def dot_nt(a, b):
    return lax.dot_general(a, b, (((1,), (1,)), ((), ())), preferred_element_type=F32)


def dot_tn(a, b):
    return lax.dot_general(a, b, (((0,), (0,)), ((), ())), preferred_element_type=F32)


def drain(ref, sem):
    pltpu.make_async_copy(ref, ref, sem).wait()


def kernel(
    act, cot, gate_t, up_t, down, spread, spread_t,
    gate_out, up_out, down_out, inner_out, direct_out,
    experts, tokens, merged, weights, terms, part_out, part_in, deltas,
    direct, from_pair, to_depth, from_depth, depth_sum, to_owner, direct_all, inner,
    e_sem, tok_sem, tok_send, pass_send, m_send, m_recv, p_send, p_recv, d_send, d_recv,
    t_send, t_recv, s_send, s_recv, z_send, z_recv, o_send, o_recv, a_send, a_recv,
    f_send, f_recv, out_sem,
):
    row = lax.axis_index("row")
    col = lax.axis_index("col")
    x, y = row // SIDE, row % SIDE
    z, k = col // 2, col % 2
    sibling = (row, z * 2 + 1 - k)

    def line(h, at):
        return jnp.where(h == 0, at * SIDE + y, x * SIDE + at)

    def cross(h, at):
        return jnp.where(h == 0, x * SIDE + at, at * SIDE + y)

    def send(src, dst, send_sem, recv_sem, to):
        pltpu.make_async_remote_copy(
            src_ref=src, dst_ref=dst, send_sem=send_sem, recv_sem=recv_sem,
            device_id=to, device_id_type=MESH,
        ).start()

    loads = [
        pltpu.make_async_copy(src, experts.at[:, :, pl.ds(n * BLOCK, BLOCK)], e_sem.at[n])
        for n, src in enumerate((gate_t, up_t, down))
    ]
    for load in loads:
        load.start()

    peers = []
    for o in range(1, SIDE):
        peers.append((((x + o) % SIDE) * SIDE + y, col))
        peers.append((x * SIDE + (y + o) % SIDE, col))
    for o in range(1, DEPTH):
        peers.append((row, ((z + o) % DEPTH) * 2 + k))
    peers.append(sibling)
    barrier = pltpu.get_barrier_semaphore()
    for peer in peers:
        pl.semaphore_signal(barrier, inc=1, device_id=peer, device_id_type=MESH)
    pl.semaphore_wait(barrier, len(peers))

    mine = pl.multiple_of(k * SEG, SEG)
    for o in range(1, SIDE):
        to = (x + o) % SIDE
        for n, src in enumerate((act, cot)):
            send(
                src.at[pl.ds(mine, SEG), pl.ds(pl.multiple_of(to * WIDE, WIDE), WIDE)],
                tokens.at[0, SIDE * k + x, n],
                tok_send.at[0, o - 1], tok_sem.at[0, SIDE * k + x], (to * SIDE + y, col),
            )
        to = (y + o) % SIDE
        for n, src in enumerate((act, cot)):
            for q in range(SIDE):
                send(
                    src.at[pl.ds(mine, SEG), pl.ds(pl.multiple_of((q * SIDE + to) * BLOCK, BLOCK), BLOCK)],
                    tokens.at[1, SIDE * k + y, n, :, pl.ds(q * BLOCK, BLOCK)],
                    tok_send.at[1, o - 1], tok_sem.at[1, SIDE * k + y], (x * SIDE + to, col),
                )
    for b in range(2):
        rows = pl.ds(b * SEG, SEG)
        for n, src in enumerate((act, cot)):
            pltpu.make_async_copy(
                src.at[rows, pl.ds(pl.multiple_of(x * WIDE, WIDE), WIDE)],
                tokens.at[0, SIDE * b + x, n], tok_sem.at[0, SIDE * b + x],
            ).start()
            for q in range(SIDE):
                pltpu.make_async_copy(
                    src.at[rows, pl.ds(pl.multiple_of((q * SIDE + y) * BLOCK, BLOCK), BLOCK)],
                    tokens.at[1, SIDE * b + y, n, :, pl.ds(q * BLOCK, BLOCK)],
                    tok_sem.at[1, SIDE * b + y],
                ).start()
    for load in loads:
        load.wait()

    for b in range(2):
        for h in range(2):

            @pl.loop(0, HALF // GROUP)
            def _(g):
                at = pl.multiple_of(g * GROUP, GROUP)
                chunk = experts[:, pl.ds(h * HALF + at, GROUP), :].reshape(EXPERTS * GROUP, LANES)
                out = dot_nn(spread[b], chunk).astype(BF16)
                merged[h, b, :, pl.ds(at, GROUP), :] = out.reshape(SIDE * SIDE, GROUP, LANES)

            own = x if h == 0 else y
            side = y if h == 0 else x

            @pl.loop(0, SIDE)
            def _(t):
                q = (own + 1 + t) % SIDE
                for o in range(SIDE):
                    to = (side + o) % SIDE
                    slot = q * SIDE + to if h == 0 else to * SIDE + q
                    src = merged.at[h, b, slot]
                    dst = weights.at[h, SIDE * b + q, side]
                    if o == 0:
                        pltpu.make_async_copy(src, dst, m_recv.at[h, SIDE * b + q]).start()
                    else:
                        device = x * SIDE + to if h == 0 else to * SIDE + y
                        send(src, dst, m_send.at[h, b], m_recv.at[h, SIDE * b + q], (device, col))

    for o in range(1, SIDE):
        for h in range(2):
            own = x if h == 0 else y
            j = SIDE * k + (own + o) % SIDE
            drain(tokens.at[h, j], tok_sem.at[h, j])
            send(tokens.at[h, j], tokens.at[h, j], pass_send.at[h, o - 1], tok_sem.at[h, j], sibling)
    for h in range(2):
        own = x if h == 0 else y
        for b in range(2):
            drain(tokens.at[h, SIDE * b + own], tok_sem.at[h, SIDE * b + own])
        for o in range(1, SIDE):
            j = SIDE * (1 - k) + (own + o) % SIDE
            drain(tokens.at[h, j], tok_sem.at[h, j])

    def joined(h, j, n):
        return jnp.concatenate(
            [weights[h, j, q, :, n * BLOCK:(n + 1) * BLOCK] for q in range(SIDE)], axis=1
        )

    @pl.loop(0, 16)
    def _(i):
        b, t, h = i // 8, (i // 2) % SIDE, i % 2
        own = jnp.where(h == 0, x, y)
        q = (own + 1 + t) % SIDE
        j = SIDE * b + q
        drain(weights.at[h, j], m_recv.at[h, j])
        for n in range(3):
            side = tokens[h, j, 0 if n < 2 else 1]
            part_out[h, j, n] = dot_nt(joined(h, j, n), side).astype(BF16)

        @pl.when(t < SIDE - 1)
        def _():
            send(part_out.at[h, j], part_in.at[h, b, t], p_send.at[h, j], p_recv.at[h, b], (line(h, q), col))

    @pl.loop(0, 4)
    def _(i):
        b, h = i // 2, i % 2
        own = jnp.where(h == 0, x, y)
        j = SIDE * b + own
        drain(part_in.at[h, b], p_recv.at[h, b])

        def total(n):
            out = part_out[h, j, n].astype(F32)
            for o in range(SIDE - 1):
                out += part_in[h, b, o, n].astype(F32)
            return out

        gate, up, grad = total(0), total(1), total(2)
        sig = jax.nn.sigmoid(gate)
        gated = gate * sig
        deltas[h, j, 0] = (grad * up * sig * (1.0 + gate * (1.0 - sig))).astype(BF16)
        deltas[h, j, 1] = (grad * gated).astype(BF16)
        deltas[h, j, 2] = (gated * up).astype(BF16)
        for o in range(1, SIDE):
            send(
                deltas.at[h, j], deltas.at[h, j], d_send.at[h, b], d_recv.at[h, j],
                (line(h, (own + o) % SIDE), col),
            )

    def item(i):
        b, t, h = i // 8, (i // 2) % SIDE, i % 2
        own = jnp.where(h == 0, x, y)
        q = (own + t) % SIDE
        return b, t, h, q, SIDE * b + q

    def pair_sum(i):
        b, t, h, q, j = item(i)
        drain(from_pair.at[h, j], s_recv.at[h, j])
        out = direct[i % 4, k].astype(F32) + from_pair[h, j].astype(F32)
        to_depth[h, j] = out.astype(BF16).reshape(DEPTH, CHUNK, WIDE)

        @pl.loop(1, DEPTH)
        def _(o):
            to = (z + o) % DEPTH
            send(
                to_depth.at[h, j, to], from_depth.at[h, j, o - 1], z_send.at[h, j], z_recv.at[h, j],
                (row, to * 2 + k),
            )

    @pl.loop(0, 16)
    def _(i):
        b, t, h, q, j = item(i)

        @pl.when(t > 0)
        def _():
            drain(deltas.at[h, j], d_recv.at[h, j])

        @pl.when(i >= 4)
        def _():
            drain(direct.at[0, 0], s_send.at[i % 4])

        both = deltas[h, j, 0:2].reshape(2 * HALF, SEG)
        out = dot_tn(both, jnp.concatenate([joined(h, j, 0), joined(h, j, 1)], axis=0))
        direct[i % 4] = out.astype(BF16).reshape(2, SEG // 2, WIDE)
        send(direct.at[i % 4, 1 - k], from_pair.at[h, j], s_send.at[i % 4], s_recv.at[h, j], sibling)

        for n in range(3):
            side = tokens[h, j, 0 if n < 2 else 1]
            out = dot_nn(deltas[h, j, n], side).astype(BF16)
            for p in range(SIDE):
                weights[h, j, p, :, n * BLOCK:(n + 1) * BLOCK] = out[:, p * BLOCK:(p + 1) * BLOCK]
        side = jnp.where(h == 0, y, x)
        slot = jnp.where(h == 0, q * SIDE + y, x * SIDE + q)
        for o in range(1, SIDE):
            to = (side + o) % SIDE
            send(
                weights.at[h, j, to], terms.at[h, b, slot], t_send.at[h, j], t_recv.at[h, b],
                (cross(h, to), col),
            )
        pltpu.make_async_copy(weights.at[h, j, side], terms.at[h, b, slot], t_recv.at[h, b]).start()

        @pl.when(i > 0)
        def _():
            pair_sum(i - 1)

    pair_sum(15)

    @pl.loop(0, 16)
    def _(i):
        b, t, h, q, j = item(i)
        drain(from_depth.at[h, j], z_recv.at[h, j])
        out = to_depth[h, j, z].astype(F32)
        for o in range(DEPTH - 1):
            out += from_depth[h, j, o].astype(F32)
        depth_sum[h, j] = out.astype(BF16)
        own = jnp.where(h == 0, x, y)

        @pl.when(t == 0)
        def _():
            to_owner[h, b, own] = out.astype(BF16)

        @pl.when(t > 0)
        def _():
            send(
                depth_sum.at[h, j], to_owner.at[h, b, own], o_send.at[h, b], o_recv.at[h, b],
                (line(h, q), col),
            )

    for n in range(2):
        inner[n] = jnp.zeros((EXPERTS * GROUP, EXPERTS * GROUP), F32)
    for h in range(2):
        for b in range(2):
            drain(terms.at[h, b], t_recv.at[h, b])
            drain(merged.at[h, b, 0:12], m_send.at[h, b])

    def gradients(h):
        @pl.loop(0, HALF // GROUP)
        def _(g):
            at = pl.multiple_of(g * GROUP, GROUP)
            chunk = experts[:, pl.ds(h * HALF + at, GROUP), :].reshape(EXPERTS * GROUP, LANES)
            out = None
            for b in range(2):
                term = terms[h, b, :, pl.ds(at, GROUP), :].reshape(EXPERTS * GROUP, LANES)
                part = dot_nn(spread_t[b], term)
                out = part if out is None else out + part
                inner[b] += dot_nt(term, chunk)
            merged[h, 0, :, pl.ds(at, GROUP), :] = out.astype(BF16).reshape(EXPERTS, GROUP, LANES)

        for n, dst in enumerate((gate_out, up_out, down_out)):
            pltpu.make_async_copy(
                merged.at[h, 0, :, :, pl.ds(n * BLOCK, BLOCK)],
                dst.at[:, pl.ds(h * HALF, HALF), :], out_sem.at[h, n],
            ).start()

    gradients(0)

    place = pl.ds(pl.multiple_of(k * (SEG // 2) + z * CHUNK, CHUNK), CHUNK)
    for b in range(2):
        for h in range(2):
            drain(to_owner.at[h, b, 0:3], o_recv.at[h, b])
        pieces = []
        for p in range(SIDE):
            for q in range(SIDE):
                one = to_owner[0, b, p, :, q * BLOCK:(q + 1) * BLOCK].astype(F32)
                two = to_owner[1, b, q, :, p * BLOCK:(p + 1) * BLOCK].astype(F32)
                pieces.append((one + two).astype(BF16))
        direct_all[b, place, :] = jnp.concatenate(pieces, axis=1)

        @pl.loop(1, DEPTH)
        def _(o):
            to = (z + o) % DEPTH
            send(
                direct_all.at[b, place], direct_all.at[b, place], a_send.at[b], a_recv.at[b],
                (row, to * 2 + k),
            )

    gradients(1)

    half = pl.ds(pl.multiple_of(k * (SEG // 2), SEG // 2), SEG // 2)
    for b in range(2):
        drain(direct_all.at[b, 0:7 * CHUNK], a_recv.at[b])
        send(direct_all.at[b, half], direct_all.at[b, half], f_send.at[b], f_recv.at[b], sibling)

    rows = lax.broadcasted_iota(jnp.int32, (EXPERTS * GROUP, EXPERTS * GROUP), 0)
    cols = lax.broadcasted_iota(jnp.int32, (EXPERTS * GROUP, EXPERTS * GROUP), 1)
    same = rows % GROUP == cols % GROUP
    for b in range(2):
        kept = jnp.where(same, inner[b], 0.0)
        inner_out[b] = jnp.sum(kept.reshape(EXPERTS, GROUP, EXPERTS * GROUP), axis=1)

    for b in range(2):
        drain(direct_all.at[b, 0:SEG // 2], f_recv.at[b])
    copy = pltpu.make_async_copy(direct_all, direct_out, e_sem.at[0])
    copy.start()

    for h in range(2):
        for o in range(SIDE - 1):
            drain(tokens.at[h, 0], tok_send.at[h, o])
            drain(tokens.at[h, 0], pass_send.at[h, o])
        for b in range(2):
            drain(deltas.at[h, 0:3], d_send.at[h, b])
            drain(depth_sum.at[h, 0:3], o_send.at[h, b])
        own = x if h == 0 else y

        @pl.loop(0, 8)
        def _(j):
            @pl.when(j % SIDE != own)
            def _():
                drain(part_out.at[h, 0], p_send.at[h, j])

            drain(weights.at[h, 0, 0:3], t_send.at[h, j])
            drain(to_depth.at[h, 0, 0:7], z_send.at[h, j])

        for n in range(3):
            drain(merged.at[h, 0, :, :, pl.ds(n * BLOCK, BLOCK)], out_sem.at[h, n])
    for n in range(4):
        drain(direct.at[0, 0], s_send.at[n])
    for b in range(2):
        drain(direct_all.at[b, 0:7 * CHUNK], a_send.at[b])
        drain(direct_all.at[b, 0:SEG // 2], f_send.at[b])
    copy.wait()


def moved(act, cot, gate_t, up_t, down, spread, spread_t):
    units = gate_t.shape[1]
    grad = jax.ShapeDtypeStruct((EXPERTS, units, BLOCK), BF16)
    vmem = pl.BlockSpec(memory_space=pltpu.VMEM)
    anywhere = pl.BlockSpec(memory_space=pl.ANY)
    dma = pltpu.SemaphoreType.DMA
    segs = SIDE * SIDE
    return pl.pallas_call(
        kernel,
        out_shape=(
            grad, grad, grad,
            jax.ShapeDtypeStruct((2, EXPERTS, EXPERTS * GROUP), F32),
            jax.ShapeDtypeStruct((2, SEG, 4 * WIDE), BF16),
        ),
        in_specs=[anywhere] * 5 + [vmem] * 2,
        out_specs=(anywhere, anywhere, anywhere, vmem, anywhere),
        scratch_shapes=[
            pltpu.VMEM((EXPERTS, 2 * HALF, LANES), BF16),
            pltpu.VMEM((2, 8, 2, SEG, WIDE), BF16),
            pltpu.VMEM((2, 2, segs, HALF, LANES), BF16),
            pltpu.VMEM((2, 8, SIDE, HALF, LANES), BF16),
            pltpu.VMEM((2, 2, segs, HALF, LANES), BF16),
            pltpu.VMEM((2, 8, 3, HALF, SEG), BF16),
            pltpu.VMEM((2, 2, 3, 3, HALF, SEG), BF16),
            pltpu.VMEM((2, 8, 3, HALF, SEG), BF16),
            pltpu.VMEM((4, 2, SEG // 2, WIDE), BF16),
            pltpu.VMEM((2, 8, SEG // 2, WIDE), BF16),
            pltpu.VMEM((2, 8, DEPTH, CHUNK, WIDE), BF16),
            pltpu.VMEM((2, 8, DEPTH - 1, CHUNK, WIDE), BF16),
            pltpu.VMEM((2, 8, CHUNK, WIDE), BF16),
            pltpu.VMEM((2, 2, SIDE, CHUNK, WIDE), BF16),
            pltpu.VMEM((2, SEG, 4 * WIDE), BF16),
            pltpu.VMEM((2, EXPERTS * GROUP, EXPERTS * GROUP), F32),
            dma((3,)), dma((2, 8)), dma((2, 3)), dma((2, 3)),
            dma((2, 2)), dma((2, 8)), dma((2, 8)), dma((2, 2)), dma((2, 2)), dma((2, 8)),
            dma((2, 8)), dma((2, 2)), dma((4,)), dma((2, 8)), dma((2, 8)), dma((2, 8)),
            dma((2, 2)), dma((2, 2)), dma((2,)), dma((2,)), dma((2,)), dma((2,)), dma((2, 3)),
        ],
        compiler_params=pltpu.CompilerParams(
            collective_id=1, has_side_effects=True, vmem_limit_bytes=63 * 2**20
        ),
        cost_estimate=pl.CostEstimate(flops=12 * 10**9, bytes_accessed=16 * 10**6, transcendentals=0),
        name="experts",
    )(act, cot, gate_t, up_t, down, spread, spread_t)


def shards(activations, cotangent, router, gate_experts, up_experts, down_experts, route_source):
    model_width = activations.shape[1]
    segs_here = activations.shape[0] // SEG
    seg_count = segs_here * lax.axis_size("row")
    first_seg = lax.axis_index("row") * segs_here
    own_means = jnp.mean(activations.reshape(segs_here, SEG, model_width), axis=1, dtype=F32)
    all_means = lax.all_gather(own_means, "row", axis=0, tiled=True)
    all_scores = jnp.dot(all_means, router, precision=PRECISE)
    chooser = (route_source[:, None] == jnp.arange(seg_count, dtype=jnp.int32)[None, :]).astype(F32)
    logits = jnp.dot(chooser, all_scores, precision=PRECISE)
    powers = jnp.exp(logits)
    routes = powers / jnp.sum(powers, axis=-1, keepdims=True)
    rounded = routes.astype(BF16)
    ordered = rounded.reshape(seg_count // 2, 2, EXPERTS).transpose(1, 0, 2)
    same = jnp.eye(GROUP, dtype=BF16)
    wide = EXPERTS * GROUP
    spread = (ordered[:, :, None, :, None] * same[None, None, :, None, :]).reshape(2, wide, wide)
    spread_t = spread.transpose(0, 2, 1)
    gate_t, up_t, down_t, inner, direct = moved(
        activations, cotangent, gate_experts.transpose(0, 2, 1), up_experts.transpose(0, 2, 1),
        down_experts, spread, spread_t,
    )
    partial_value = jnp.sum(inner.reshape(2, seg_count // 2, EXPERTS, GROUP), axis=-1)
    partial_value = partial_value.transpose(1, 0, 2).reshape(seg_count, EXPERTS)
    route_grad = lax.psum(partial_value, ("row", "col"))
    logit_grad = routes * (route_grad - jnp.sum(routes * route_grad, axis=-1, keepdims=True))
    source_grad = jnp.dot(chooser.T, logit_grad, precision=PRECISE)
    own_source = lax.dynamic_slice_in_dim(source_grad, first_seg, segs_here, 0)
    router_grad = jnp.dot(all_means.T, source_grad, precision=PRECISE)
    mean_grad = jnp.dot(own_source, router.T, precision=PRECISE)
    input_grad = (
        (direct.astype(F32) + mean_grad[:, None, :] / SEG).reshape(-1, model_width).astype(BF16)
    )
    return (
        input_grad, gate_t.transpose(0, 2, 1), up_t.transpose(0, 2, 1), down_t, router_grad,
    )


def solution(mesh):
    in_specs = (
        P("row", None),
        P("row", None),
        P(),
        P(None, "row", "col"),
        P(None, "row", "col"),
        P(None, "col", "row"),
        P(),
    )
    out_specs = (
        P("row", None),
        P(None, "row", "col"),
        P(None, "row", "col"),
        P(None, "col", "row"),
        P(),
    )
    return jax.shard_map(shards, mesh=mesh, in_specs=in_specs, out_specs=out_specs, check_vma=False)
```

time: 412 us -> 326 us (0.79)
  Pallas kernels: 0 us -> 211 us
  local copies, waits for them, and re-layouts: 111 us -> 10.6 us
  waiting for transfers between devices: 85.3 us -> 0 us
  starting transfers between devices: 48.6 us -> 0 us
  matrix products: 39.6 us -> 2.01 us
  between operations: 14.4 us -> 0.78 us
  blocking collectives: 104 us -> 95 us
    pallas_call x0 -> x1, Pallas kernels: none -> 211 us  [moved(): pl.pallas_call(kernel, out_shape=(grad, grad, grad, jax.ShapeDtypeStruct(...]
    all_to_all x6 -> x0, waiting for transfers between devices: 85.2 us -> none  [the longest x1 28.1 us: shards(): lax.all_to_all(local_gate, 'row', split_axis=0, concat_axis=1, tiled=True)]
    all_to_all x9 -> x0, local copies, waits for them, and re-layouts: 66.1 us -> none  [the longest x1 11.2 us: shards(): lax.all_to_all(up_own, 'row', split_axis=1, concat_axis=0, tiled=True)]
    all_to_all x6 -> x0, starting transfers between devices: 48.3 us -> none  [the longest x1 10.8 us: shards(): lax.all_to_all(up_own, 'row', split_axis=1, concat_axis=0, tiled=True)]
    dot_general x17 -> x0, matrix products: 36.6 us -> none  [the longest x1 4.19 us: shards(): jnp.einsum('wzp,wpg->wzg', output_gradients, combined_down_weight, prefer...]
    convert_element_type x6 -> x1, local copies, waits for them, and re-layouts: 34.3 us -> 0.09 us  [shards(): rounded = routes.astype(BF16)]
    psum x1, blocking collectives: 82.6 us -> 75.3 us  [shards(): route_grad = lax.psum(partial_value, ('row', 'col'))]
    unnamed x52 -> x14, local copies, waits for them, and re-layouts: 10.8 us -> 5.06 us
  transfers between devices with their start and end apart: 7 -> 0, of which waited for: 4 -> 0; matrix products, arithmetic and copies ran while one was open for 30% -> 0% of each run, Pallas kernels for 0% -> 0%
where the time goes in v1:
time: 326 us
  Pallas kernels  211 us (65%)
  blocking collectives  95 us (29%)
  local copies, waits for them, and re-layouts  10.6 us (3%)
  other arithmetic  6.53 us (2%)
    pallas_call x1, Pallas kernels, moved(): pl.pallas_call(kernel, out_shape=(grad, grad, grad, jax.ShapeDtypeStruct(...  211 us
    psum x1, blocking collectives, shards(): route_grad = lax.psum(partial_value, ('row', 'col'))  75.3 us
    all_gather x1, blocking collectives, shards(): all_means = lax.all_gather(own_means, 'row', axis=0, tiled=True)  19.7 us

profile of v1, /device:TPU:1, one launch (start us, length us, event | category | flops | bytes accessed | tf_op | source)
XLA Modules:
  0.0 326.0 jit_solution(1070969631757438330)
XLA Ops:
  0.6 0.0 copy-start
  0.6 0.0 copy-start.4
  0.7 2.0 convert_reduce_fusion
  2.7 19.7 %all-gather = f32[16,2,2048]{2,1,0:T(2,128)S(1)} all-gather(f32[1,2,2048]{2,1,0:T(2,128)S(1)} %multiply_bitcast_fusion), channel_id=1, replica_groups=mesh['row'=16,'col'=16] {'row'}, dimensions={0}, use_global_device_ids=true | all-gather | bytes 278528 | tf_op jit(solution)/shard_map/all_gather | solution.py:433
  22.4 0.2 reshape.46
  22.6 0.0 copy-done
  22.6 0.3 fusion.11
  22.9 0.0 copy-done.4
  22.9 0.3 fusion.10
  23.2 0.1 copy.18
  23.2 0.1 copy.19
  23.3 0.2 mul.31
  23.6 1.0 mul.32
  24.5 0.3 mul.29
  24.9 2.0 mul.30
  26.9 0.7 fusion.19.spread_t
  27.7 0.8 copy.20.spread
  28.5 211.1 %experts.1 = (bf16[16,352,128]{2,1,0:T(8,128)(2,1)}, bf16[16,352,128]{2,1,0:T(8,128)(2,1)}, bf16[16,352,128]{2,1,0:T(8,128)(2,1)}, f32[2,16,256]{2,1,0:T(8,128)}, bf16[2,256,2048]{2,1,0:T(8,128)(2,1)}) custom-call(bf16[512,2048]{1,0:T(8,128)(2,1)} %act.1, bf16[512,2048]{1,0:T(8,128)(2,1)} %cot.1, bf16[16,352,128]{2,1,0:T(8,128)(2,1)} %bitcast.37, ...), custom_call_target="tpu_custom_call" | custom-call | flops 12000000000 | bytes 16000000 | tf_op jit(solution)/shard_map/experts/pallas_call | solution.py:388
  239.6 0.9 reshape.42
  240.5 0.1 reduce_sum.38
  240.7 0.1 copy.22
  240.8 75.3 %psum.7 = f32[32,16]{0,1:T(8,128)S(1)} all-reduce(f32[32,16]{0,1:T(8,128)S(1)} %copy.22), channel_id=1, replica_groups=mesh['row'=16,'col'=16] {'row','col'}, use_global_device_ids=true, to_apply=%region_3.0 | all-reduce | flops 512 | bytes 4096 | tf_op jit(solution)/shard_map/psum | solution.py:451
  316.1 0.2 fusion
  316.3 1.0 fusion.12
  317.2 0.3 convolution_multiply_fusion
  317.5 0.0 copy-start.3
  317.6 3.6 %add_convert_fusion = bf16[2,256,2048]{2,1,0:T(8,128)(2,1)} fusion(bf16[2,256,2048]{2,1,0:T(8,128)(2,1)} %get-tuple-element.10, f32[2,2048]{1,0:T(2,128)S(1)} %convolution_multiply_fusion), kind=kLoop, calls=%fused_computation.1 | loop fusion | flops 3145728 | bytes 4210688 | tf_op jit(solution)/shard_map/convert_element_type | solution.py:458
  321.1 1.1 copy.26
  322.2 0.8 copy-done.2
  323.0 1.1 copy.27
  324.1 0.8 copy-done.1
  324.9 1.1 copy.28
  (9 shorter events, 0.1 us)
Async XLA Ops:
  0.6 21.9 %copy-start = (f32[2048,16]{0,1:T(8,128)S(1)}, f32[2048,16]{0,1:T(8,128)}, u32[]{:S(2)}) copy-start(f32[2048,16]{0,1:T(8,128)} %param.9) | copy-start | bytes 393220
  0.6 22.2 %copy-start.4 = (s32[32]{0:T(128)S(1)}, s32[32]{0:T(128)}, u32[]{:S(2)}) copy-start(s32[32]{0:T(128)} %param.13) | copy-start | bytes 388
  317.5 3.6 %copy-start.3 = (bf16[16,352,128]{2,1,0:T(8,128)(2,1)S(1)}, bf16[16,352,128]{2,1,0:T(8,128)(2,1)}, u32[]{:S(2)}) copy-start(bf16[16,352,128]{2,1,0:T(8,128)(2,1)} %get-tuple-element.12) | copy-start | bytes 4325380
  321.1 1.9 copy-start.2
  323.0 1.9 copy-start.1

commit v2 on v1

v2 whole, which is shorter than its diff:
```python
import functools

import jax
import jax.numpy as jnp
from jax import lax
from jax.experimental import pallas as pl
from jax.experimental.pallas import tpu as pltpu
from jax.sharding import PartitionSpec as P

SEG = 256
EXPERTS = 16
SIDE = 4
DEPTH = 8
BLOCK = 128
HALF = 176
LANES = 3 * BLOCK
WIDE = SIDE * BLOCK
GROUP = 16
CHUNK = 16
PIECE = 32
PRECISE = lax.Precision.HIGHEST
MESH = pl.DeviceIdType.MESH
F32 = jnp.float32
BF16 = jnp.bfloat16


def dot_nn(a, b):
    return lax.dot_general(a, b, (((1,), (0,)), ((), ())), preferred_element_type=F32)


def dot_nt(a, b):
    return lax.dot_general(a, b, (((1,), (1,)), ((), ())), preferred_element_type=F32)


def dot_tn(a, b):
    return lax.dot_general(a, b, (((0,), (0,)), ((), ())), preferred_element_type=F32)


def drain(ref, sem):
    pltpu.make_async_copy(ref, ref, sem).wait()


def kernel(
    act, cot, gate_t, up_t, down, router_t, wanted,
    gate_out, up_out, down_out, source_out, means_out, direct_out,
    experts, tokens, merged, weights, terms, part_out, part_in, deltas,
    direct, from_pair, to_depth, from_depth, depth_sum, to_owner, direct_all, inner,
    spread, spread_t, scores, means, routes, in_row, in_col, source, chooser,
    e_sem, tok_sem, tok_send, near_sem, near_send, pass_sem, pass_send, m_send, m_recv, p_send, p_recv, d_send, d_recv,
    t_send, t_recv, s_send, s_recv, z_send, z_recv, o_send, o_recv, a_send, a_recv,
    f_send, f_recv, out_sem, c_send, c_recv, n_send, n_recv, r_send, r_recv, l_send, l_recv,
):
    row = lax.axis_index("row")
    col = lax.axis_index("col")
    x, y = row // SIDE, row % SIDE
    z, k = col // 2, col % 2
    sibling = (row, z * 2 + 1 - k)

    def line(h, at):
        return jnp.where(h == 0, at * SIDE + y, x * SIDE + at)

    def cross(h, at):
        return jnp.where(h == 0, x * SIDE + at, at * SIDE + y)

    def send(src, dst, send_sem, recv_sem, to):
        pltpu.make_async_remote_copy(
            src_ref=src, dst_ref=dst, send_sem=send_sem, recv_sem=recv_sem,
            device_id=to, device_id_type=MESH,
        ).start()

    loads = [
        pltpu.make_async_copy(src, experts.at[:, :, pl.ds(n * BLOCK, BLOCK)], e_sem.at[n])
        for n, src in enumerate((gate_t, up_t, down))
    ]
    read = pltpu.make_async_copy(act, direct_all, out_sem.at[0, 0])
    read.start()
    for load in loads:
        load.start()

    rows_all = SIDE * SIDE
    cols_all = 2 * DEPTH
    barrier = pltpu.get_barrier_semaphore()

    @pl.loop(1, rows_all)
    def _(o):
        pl.semaphore_signal(
            barrier, inc=1, device_id=((row + o) % rows_all, col), device_id_type=MESH
        )

    @pl.loop(1, cols_all)
    def _(o):
        pl.semaphore_signal(
            barrier, inc=1, device_id=(row, (col + o) % cols_all), device_id_type=MESH
        )

    read.wait()
    found = []
    for b in range(2):
        def add(i, total):
            at = pl.multiple_of(b * SEG + i * GROUP, GROUP)
            return total + direct_all[pl.ds(at, GROUP), :].astype(F32)

        total = lax.fori_loop(0, SEG // GROUP, add, jnp.zeros((GROUP, 4 * WIDE), F32))
        found.append(jnp.sum(total, axis=0, keepdims=True) / SEG)
        for q in range(rows_all):
            means[row, b * rows_all + q:b * rows_all + q + 1, :] = found[b][:, q * BLOCK:(q + 1) * BLOCK]
    found.append(jnp.zeros((6, 4 * WIDE), F32))
    scores[row] = jnp.zeros((8, BLOCK), F32)
    scores[row, :, 0:EXPERTS] = lax.dot_general(
        jnp.concatenate(found, axis=0), router_t[...], (((1,), (1,)), ((), ())),
        precision=PRECISE, preferred_element_type=F32,
    )
    pl.semaphore_wait(barrier, rows_all + cols_all - 2)

    @pl.loop(1, rows_all)
    def _(o):
        send(scores.at[row], scores.at[row], c_send, c_recv, ((row + o) % rows_all, col))

    first = pl.multiple_of((k * SIDE + z % SIDE) * PIECE, PIECE)
    piece = pl.ds(first, PIECE)

    @pl.loop(0, 2)
    def _(b):
        rows = pl.ds(pl.multiple_of(b * SEG + first, PIECE), PIECE)
        for o in range(1, SIDE):
            for n, src in enumerate((act, cot)):
                to = (x + o) % SIDE
                j = SIDE * b + x
                send(
                    src.at[rows, pl.ds(pl.multiple_of(to * WIDE, WIDE), WIDE)],
                    tokens.at[0, j, n, piece], tok_send, tok_sem.at[0, j], (to * SIDE + y, col),
                )
                to = (y + o) % SIDE
                j = SIDE * b + y
                for q in range(SIDE):
                    send(
                        src.at[rows, pl.ds(pl.multiple_of((q * SIDE + to) * BLOCK, BLOCK), BLOCK)],
                        tokens.at[1, j, n, piece, pl.ds(q * BLOCK, BLOCK)],
                        tok_send, tok_sem.at[1, j], (x * SIDE + to, col),
                    )

    for b in range(2):
        rows = pl.ds(b * SEG, SEG)
        for n, src in enumerate((act, cot)):
            pltpu.make_async_copy(
                src.at[rows, pl.ds(pl.multiple_of(x * WIDE, WIDE), WIDE)],
                tokens.at[0, SIDE * b + x, n], tok_sem.at[0, SIDE * b + x],
            ).start()
            for q in range(SIDE):
                pltpu.make_async_copy(
                    src.at[rows, pl.ds(pl.multiple_of((q * SIDE + y) * BLOCK, BLOCK), BLOCK)],
                    tokens.at[1, SIDE * b + y, n, :, pl.ds(q * BLOCK, BLOCK)],
                    tok_sem.at[1, SIDE * b + y],
                ).start()
    for s in range(2 * rows_all):
        at = (s % 2) * rows_all + s // 2
        v = wanted[s]
        place = (v // 2) * 8 + v % 2
        lanes = lax.broadcasted_iota(jnp.int32, (1, BLOCK), 1)
        chooser[at:at + 1, :] = jnp.where(lanes == place, 1.0, 0.0).astype(F32)

    drain(scores.at[0:rows_all - 1], c_recv)
    logits = lax.dot_general(
        chooser[...], scores[...].reshape(rows_all * 8, BLOCK), (((1,), (0,)), ((), ())),
        precision=PRECISE, preferred_element_type=F32,
    )
    real = lax.broadcasted_iota(jnp.int32, logits.shape, 1) < EXPERTS
    powers = jnp.where(real, jnp.exp(logits), 0.0)
    routes[...] = powers / jnp.sum(powers, axis=1, keepdims=True)
    span = EXPERTS * GROUP

    def iota(shape, axis):
        return lax.broadcasted_iota(jnp.int32, shape, axis)

    same = iota((span, span), 0) % GROUP == iota((span, span), 1) % GROUP
    pick = (iota((span, rows_all), 0) // GROUP == iota((span, rows_all), 1)).astype(BF16)
    expand = (iota((span, BLOCK), 0) // GROUP == iota((span, BLOCK), 1)).astype(BF16)
    for b in range(2):
        rounded = routes[b * rows_all:(b + 1) * rows_all, :].astype(BF16)
        long = dot_nt(dot_nn(pick, rounded).astype(BF16), expand)
        spread[b] = jnp.where(same, long, 0.0).astype(BF16)
        long = dot_nt(dot_nt(expand, rounded).astype(BF16), pick)
        spread_t[b] = jnp.where(same, long, 0.0).astype(BF16)

    def others(b, h):
        own = x if h == 0 else y
        return [SIDE * b + (own + o) % SIDE for o in range(1, SIDE)]

    for b in range(2):
        for o in range(SIDE - 1):
            for h in range(2):
                j = others(b, h)[o]
                drain(tokens.at[0, 0, :, 0:PIECE], tok_sem.at[h, j])
                both = tokens.at[h, j, :, piece]
                for step in (1, DEPTH - 1):
                    to = (row, (z + step) % DEPTH * 2 + k)
                    send(both, both, near_send.at[0], near_sem.at[h, j], to)
                for n, step in enumerate((2, DEPTH - 2)):
                    one = tokens.at[h, j, n, piece]
                    to = (row, (z + step) % DEPTH * 2 + k)
                    send(one, one, near_send.at[1], near_sem.at[h, j], to)
    for load in loads:
        load.wait()

    for b in range(2):
        for h in range(2):

            @pl.loop(0, HALF // GROUP)
            def _(g):
                at = pl.multiple_of(g * GROUP, GROUP)
                chunk = experts[:, pl.ds(h * HALF + at, GROUP), :].reshape(EXPERTS * GROUP, LANES)
                out = dot_nn(spread[b], chunk).astype(BF16)
                merged[h, b, :, pl.ds(at, GROUP), :] = out.reshape(SIDE * SIDE, GROUP, LANES)

            own = x if h == 0 else y
            side = y if h == 0 else x

            @pl.loop(0, SIDE)
            def _(t):
                q = (own + 1 + t) % SIDE
                for o in range(SIDE):
                    to = (side + o) % SIDE
                    slot = q * SIDE + to if h == 0 else to * SIDE + q
                    src = merged.at[h, b, slot]
                    dst = weights.at[h, SIDE * b + q, side]
                    if o == 0:
                        pltpu.make_async_copy(src, dst, m_recv.at[h, SIDE * b + q]).start()
                    else:
                        device = x * SIDE + to if h == 0 else to * SIDE + y
                        send(src, dst, m_send.at[h, b], m_recv.at[h, SIDE * b + q], (device, col))

    def joined(h, j, n):
        return jnp.concatenate(
            [weights[h, j, q, :, n * BLOCK:(n + 1) * BLOCK] for q in range(SIDE)], axis=1
        )

    def forward(b):
        own_half = pl.ds(pl.multiple_of(k * (SEG // 2), SEG // 2), SEG // 2)
        for o in range(SIDE - 1):
            for h in range(2):
                j = others(b, h)[o]
                drain(tokens.at[0, 0, :, 0:3 * PIECE], near_sem.at[h, j])
                part = tokens.at[h, j, :, own_half]
                send(part, part, pass_send.at[b], pass_sem.at[h, j], sibling)

        @pl.loop(0, 8)
        def _(i):
            t, h = i // 2, i % 2
            own = jnp.where(h == 0, x, y)
            q = (own + 1 + t) % SIDE
            j = SIDE * b + q
            drain(weights.at[h, j], m_recv.at[h, j])

            @pl.when(t < SIDE - 1)
            def _():
                drain(tokens.at[0, 0, :, 0:SEG // 2], pass_sem.at[h, j])

            @pl.when(t == SIDE - 1)
            def _():
                drain(tokens.at[h, j], tok_sem.at[h, j])

            for n in range(3):
                side = tokens[h, j, 0 if n < 2 else 1]
                part_out[h, j, n] = dot_nt(joined(h, j, n), side).astype(BF16)

            @pl.when(t < SIDE - 1)
            def _():
                send(
                    part_out.at[h, j], part_in.at[h, b, t], p_send.at[h, j], p_recv.at[h, b],
                    (line(h, q), col),
                )

    forward(0)
    forward(1)

    @pl.loop(0, 4)
    def _(i):
        b, h = i // 2, i % 2
        own = jnp.where(h == 0, x, y)
        j = SIDE * b + own
        drain(part_in.at[h, b], p_recv.at[h, b])

        def total(n):
            out = part_out[h, j, n].astype(F32)
            for o in range(SIDE - 1):
                out += part_in[h, b, o, n].astype(F32)
            return out

        gate, up, grad = total(0), total(1), total(2)
        sig = jax.nn.sigmoid(gate)
        gated = gate * sig
        deltas[h, j, 0] = (grad * up * sig * (1.0 + gate * (1.0 - sig))).astype(BF16)
        deltas[h, j, 1] = (grad * gated).astype(BF16)
        deltas[h, j, 2] = (gated * up).astype(BF16)
        for o in range(1, SIDE):
            send(
                deltas.at[h, j], deltas.at[h, j], d_send.at[h, b], d_recv.at[h, j],
                (line(h, (own + o) % SIDE), col),
            )

    def item(i):
        b, t, h = i // 8, (i // 2) % SIDE, i % 2
        own = jnp.where(h == 0, x, y)
        q = (own + t) % SIDE
        return b, t, h, q, SIDE * b + q

    def pair_sum(i):
        b, t, h, q, j = item(i)
        drain(from_pair.at[h, j], s_recv.at[h, j])
        out = direct[i % 4, k].astype(F32) + from_pair[h, j].astype(F32)
        to_depth[h, j] = out.astype(BF16).reshape(DEPTH, CHUNK, WIDE)

        @pl.loop(1, DEPTH)
        def _(o):
            to = (z + o) % DEPTH
            send(
                to_depth.at[h, j, to], from_depth.at[h, j, o - 1], z_send.at[h, j], z_recv.at[h, j],
                (row, to * 2 + k),
            )

    def send_terms(i):
        b, t, h, q, j = item(i)
        side = jnp.where(h == 0, y, x)
        slot = jnp.where(h == 0, q * SIDE + y, x * SIDE + q)
        for o in range(1, SIDE):
            to = (side + o) % SIDE
            send(
                weights.at[h, j, to], terms.at[h, b, slot], t_send.at[h, j], t_recv.at[h, b],
                (cross(h, to), col),
            )
        pltpu.make_async_copy(weights.at[h, j, side], terms.at[h, b, slot], t_recv.at[h, b]).start()

    def backward(i):
        b, t, h, q, j = item(i)

        @pl.when(t > 0)
        def _():
            drain(deltas.at[h, j], d_recv.at[h, j])

        @pl.when(i >= 4)
        def _():
            drain(direct.at[0, 0], s_send.at[i % 4])

        both = deltas[h, j, 0:2].reshape(2 * HALF, SEG)
        out = dot_tn(both, jnp.concatenate([joined(h, j, 0), joined(h, j, 1)], axis=0))
        direct[i % 4] = out.astype(BF16).reshape(2, SEG // 2, WIDE)
        send(direct.at[i % 4, 1 - k], from_pair.at[h, j], s_send.at[i % 4], s_recv.at[h, j], sibling)

        for n in range(3):
            side = tokens[h, j, 0 if n < 2 else 1]
            out = dot_nn(deltas[h, j, n], side).astype(BF16)
            for p in range(SIDE):
                weights[h, j, p, :, n * BLOCK:(n + 1) * BLOCK] = out[:, p * BLOCK:(p + 1) * BLOCK]

        @pl.when(i > 0)
        def _():
            pair_sum(i - 1)

    @pl.loop(0, 8)
    def _(i):
        backward(i)
        send_terms(i)

    @pl.loop(8, 16)
    def _(i):
        backward(i)

    pair_sum(15)

    def depth_sums(b):
        @pl.loop(0, 8)
        def _(i):
            _, t, h, q, j = item(b * 8 + i)
            drain(from_depth.at[h, j], z_recv.at[h, j])
            out = to_depth[h, j, z].astype(F32)
            for o in range(DEPTH - 1):
                out += from_depth[h, j, o].astype(F32)
            depth_sum[h, j] = out.astype(BF16)
            own = jnp.where(h == 0, x, y)

            @pl.when(t == 0)
            def _():
                to_owner[h, b, own] = out.astype(BF16)

            @pl.when(t > 0)
            def _():
                send(
                    depth_sum.at[h, j], to_owner.at[h, b, own], o_send.at[h, b], o_recv.at[h, b],
                    (line(h, q), col),
                )

    def place(b):
        return pl.ds(pl.multiple_of(b * SEG + k * (SEG // 2) + z * CHUNK, CHUNK), CHUNK)

    def half(b):
        return pl.ds(pl.multiple_of(b * SEG + k * (SEG // 2), SEG // 2), SEG // 2)

    def spread_direct(b):
        for h in range(2):
            drain(to_owner.at[h, b, 0:3], o_recv.at[h, b])
        pieces = []
        for p in range(SIDE):
            for q in range(SIDE):
                one = to_owner[0, b, p, :, q * BLOCK:(q + 1) * BLOCK].astype(F32)
                two = to_owner[1, b, q, :, p * BLOCK:(p + 1) * BLOCK].astype(F32)
                pieces.append((one + two).astype(BF16))
        direct_all[place(b), :] = jnp.concatenate(pieces, axis=1)

        @pl.loop(1, DEPTH)
        def _(o):
            to = (z + o) % DEPTH
            send(
                direct_all.at[place(b)], direct_all.at[place(b)], a_send.at[b], a_recv.at[b],
                (row, to * 2 + k),
            )

    def share_direct(b):
        drain(direct_all.at[0:7 * CHUNK], a_recv.at[b])
        send(direct_all.at[half(b)], direct_all.at[half(b)], f_send.at[b], f_recv.at[b], sibling)

    def group(h, g):
        at = pl.multiple_of(g * GROUP, GROUP)
        return at, experts[:, pl.ds(h * HALF + at, GROUP), :].reshape(span, LANES)

    def products(b):
        inner[b] = jnp.zeros((span, span), F32)
        for h in range(2):
            drain(terms.at[h, b], t_recv.at[h, b])

            @pl.loop(0, HALF // GROUP)
            def _(g):
                at, chunk = group(h, g)
                term = terms[h, b, :, pl.ds(at, GROUP), :].reshape(span, LANES)
                inner[b] += dot_nt(term, chunk)

    def gradients(h):
        for b in range(2):
            drain(merged.at[h, b, 0:12], m_send.at[h, b])

        @pl.loop(0, HALF // GROUP)
        def _(g):
            at = pl.multiple_of(g * GROUP, GROUP)
            out = None
            for b in range(2):
                term = terms[h, b, :, pl.ds(at, GROUP), :].reshape(span, LANES)
                part = dot_nn(spread_t[b], term)
                out = part if out is None else out + part
            merged[h, 0, :, pl.ds(at, GROUP), :] = out.astype(BF16).reshape(EXPERTS, GROUP, LANES)

        for n, dst in enumerate((gate_out, up_out, down_out)):
            pltpu.make_async_copy(
                merged.at[h, 0, :, :, pl.ds(n * BLOCK, BLOCK)],
                dst.at[:, pl.ds(h * HALF, HALF), :], out_sem.at[h, n],
            ).start()

    depth_sums(0)
    pl.loop(8, 12)(send_terms)
    spread_direct(0)
    depth_sums(1)
    pl.loop(12, 16)(send_terms)
    spread_direct(1)
    share_direct(0)
    products(0)
    products(1)

    fold = (iota((span, BLOCK), 0) // GROUP == iota((span, BLOCK), 1) % EXPERTS).astype(F32)
    here = iota((rows_all, BLOCK), 1) // EXPERTS == iota((rows_all, BLOCK), 0) % 8
    packed = []
    for b in range(2):
        kept = jnp.sum(jnp.where(same, inner[b], 0.0).reshape(EXPERTS, GROUP, span), axis=1)
        dense = lax.dot_general(
            kept, fold, (((1,), (0,)), ((), ())), precision=PRECISE, preferred_element_type=F32
        )
        packed.append(jnp.sum(jnp.where(here, dense, 0.0).reshape(2, 8, BLOCK), axis=1))
    packed.append(jnp.zeros((4, BLOCK), F32))
    in_row[0] = jnp.concatenate(packed, axis=0)

    @pl.loop(1, rows_all)
    def _(o):
        send(in_row.at[0], in_row.at[o], r_send, r_recv, ((row + o) % rows_all, col))

    gradients(0)
    share_direct(1)
    drain(in_row.at[1:rows_all], r_recv)

    @pl.loop(1, rows_all)
    def _(o):
        send(means.at[row], means.at[row], n_send, n_recv, ((row + o) % rows_all, col))

    out = in_row[0]
    for o in range(1, rows_all):
        out += in_row[o]
    in_col[0] = out

    @pl.loop(1, cols_all)
    def _(o):
        send(in_col.at[0], in_col.at[o], l_send, l_recv, (row, (col + o) % cols_all))

    gradients(1)
    for b in range(2):
        drain(direct_all.at[0:SEG // 2], f_recv.at[b])
    copy = pltpu.make_async_copy(direct_all, direct_out, e_sem.at[0])
    copy.start()
    drain(in_col.at[1:cols_all], l_recv)
    out = in_col[0]
    for o in range(1, cols_all):
        out += in_col[o]
    wide = jnp.concatenate(
        [jnp.broadcast_to(out[p:p + 1, :], (8, BLOCK)) for p in range(4)], axis=0
    )
    shape = (2 * rows_all, BLOCK)
    wide = jnp.where(iota(shape, 1) // EXPERTS == iota(shape, 0) % 8, wide, 0.0)
    narrow = (iota((BLOCK, BLOCK), 0) % EXPERTS == iota((BLOCK, BLOCK), 1)).astype(F32)
    total = lax.dot_general(
        wide, narrow, (((1,), (0,)), ((), ())), precision=PRECISE, preferred_element_type=F32
    )
    logit_grad = routes[...] * (total - jnp.sum(routes[...] * total, axis=1, keepdims=True))
    source[...] = lax.dot_general(
        chooser[...], logit_grad, (((0,), (0,)), ((), ())),
        precision=PRECISE, preferred_element_type=F32,
    ).reshape(rows_all, 8, BLOCK)
    source_out[...] = source[...]
    drain(means.at[0:rows_all - 1], n_recv)
    means_out[...] = means[...]

    for h in range(2):
        for b in range(2):
            drain(deltas.at[h, 0:3], d_send.at[h, b])
            drain(depth_sum.at[h, 0:3], o_send.at[h, b])
        own = x if h == 0 else y

        @pl.loop(0, 8)
        def _(j):
            @pl.when(j % SIDE != own)
            def _():
                drain(part_out.at[h, 0], p_send.at[h, j])

            drain(weights.at[h, 0, 0:3], t_send.at[h, j])
            drain(to_depth.at[h, 0, 0:7], z_send.at[h, j])

        for n in range(3):
            drain(merged.at[h, 0, :, :, pl.ds(n * BLOCK, BLOCK)], out_sem.at[h, n])
    for n in range(4):
        drain(direct.at[0, 0], s_send.at[n])
    drain(tokens.at[0, 0:3, 0], tok_send)
    drain(tokens.at[0, 0:3], near_send.at[0])
    drain(tokens.at[0, 0:3, 0], near_send.at[1])
    for b in range(2):
        drain(tokens.at[0, 0:3], pass_send.at[b])
        drain(direct_all.at[0:7 * CHUNK], a_send.at[b])
        drain(direct_all.at[0:SEG // 2], f_send.at[b])
    drain(scores.at[0:rows_all - 1], c_send)
    drain(means.at[0:rows_all - 1], n_send)
    drain(in_row.at[1:rows_all], r_send)
    drain(in_col.at[1:cols_all], l_send)
    copy.wait()


def moved(act, cot, gate_t, up_t, down, router_t, wanted):
    units = gate_t.shape[1]
    grad = jax.ShapeDtypeStruct((EXPERTS, units, BLOCK), BF16)
    vmem = pl.BlockSpec(memory_space=pltpu.VMEM)
    anywhere = pl.BlockSpec(memory_space=pl.ANY)
    dma = pltpu.SemaphoreType.DMA
    segs = SIDE * SIDE
    return pl.pallas_call(
        kernel,
        out_shape=(
            grad, grad, grad,
            jax.ShapeDtypeStruct((segs, 8, BLOCK), F32),
            jax.ShapeDtypeStruct((segs, 2 * segs, BLOCK), F32),
            jax.ShapeDtypeStruct((2 * SEG, 4 * WIDE), BF16),
        ),
        in_specs=[anywhere] * 5 + [vmem, pl.BlockSpec(memory_space=pltpu.SMEM)],
        out_specs=(anywhere, anywhere, anywhere, vmem, vmem, anywhere),
        scratch_shapes=[
            pltpu.VMEM((EXPERTS, 2 * HALF, LANES), BF16),
            pltpu.VMEM((2, 8, 2, SEG, WIDE), BF16),
            pltpu.VMEM((2, 2, segs, HALF, LANES), BF16),
            pltpu.VMEM((2, 8, SIDE, HALF, LANES), BF16),
            pltpu.VMEM((2, 2, segs, HALF, LANES), BF16),
            pltpu.VMEM((2, 8, 3, HALF, SEG), BF16),
            pltpu.VMEM((2, 2, 3, 3, HALF, SEG), BF16),
            pltpu.VMEM((2, 8, 3, HALF, SEG), BF16),
            pltpu.VMEM((4, 2, SEG // 2, WIDE), BF16),
            pltpu.VMEM((2, 8, SEG // 2, WIDE), BF16),
            pltpu.VMEM((2, 8, DEPTH, CHUNK, WIDE), BF16),
            pltpu.VMEM((2, 8, DEPTH - 1, CHUNK, WIDE), BF16),
            pltpu.VMEM((2, 8, CHUNK, WIDE), BF16),
            pltpu.VMEM((2, 2, SIDE, CHUNK, WIDE), BF16),
            pltpu.VMEM((2 * SEG, 4 * WIDE), BF16),
            pltpu.VMEM((2, EXPERTS * GROUP, EXPERTS * GROUP), F32),
            pltpu.VMEM((2, EXPERTS * GROUP, EXPERTS * GROUP), BF16),
            pltpu.VMEM((2, EXPERTS * GROUP, EXPERTS * GROUP), BF16),
            pltpu.VMEM((segs, 8, BLOCK), F32),
            pltpu.VMEM((segs, 2 * segs, BLOCK), F32),
            pltpu.VMEM((2 * segs, BLOCK), F32),
            pltpu.VMEM((segs, 8, BLOCK), F32),
            pltpu.VMEM((2 * DEPTH, 8, BLOCK), F32),
            pltpu.VMEM((segs, 8, BLOCK), F32),
            pltpu.VMEM((2 * segs, BLOCK), F32),
            dma((3,)), dma((2, 8)), dma, dma((2, 8)), dma((2,)), dma((2, 8)), dma((2,)),
            dma((2, 2)), dma((2, 8)), dma((2, 8)), dma((2, 2)), dma((2, 2)), dma((2, 8)),
            dma((2, 8)), dma((2, 2)), dma((4,)), dma((2, 8)), dma((2, 8)), dma((2, 8)),
            dma((2, 2)), dma((2, 2)), dma((2,)), dma((2,)), dma((2,)), dma((2,)), dma((2, 3)),
            dma, dma, dma, dma, dma, dma, dma, dma,
        ],
        compiler_params=pltpu.CompilerParams(
            collective_id=1, has_side_effects=True, vmem_limit_bytes=63 * 2**20
        ),
        cost_estimate=pl.CostEstimate(flops=12 * 10**9, bytes_accessed=16 * 10**6, transcendentals=0),
        name="experts",
    )(act, cot, gate_t, up_t, down, router_t, wanted)


def finish_kernel(
    gate, up, down, direct, source, means, router_t,
    gate_out, up_out, down_out, input_out, router_out, grads, rows, in_sem, out_sem,
):
    parts = in_sem.shape[1]
    pairs = ((gate, gate_out), (up, up_out), (down, down_out))

    def pieces(n, p, size):
        at = pl.ds(p * (size // parts), size // parts)
        if n == 3:
            return direct.at[at], rows.at[at], input_out.at[at]
        return pairs[n][0].at[at], grads.at[n, at], pairs[n][1].at[at]

    sizes = [EXPERTS] * 3 + [rows.shape[0]]
    order = [(n, p) for p in range(parts) for n in (3, 0, 1, 2)]
    for n, p in order:
        src, mid, _ = pieces(n, p, sizes[n])
        pltpu.make_async_copy(src, mid, in_sem.at[n, p]).start()
    own = source[lax.axis_index("row")]
    mean_grad = lax.dot_general(
        own[:, 0:EXPERTS], router_t[...], (((1,), (0,)), ((), ())),
        precision=PRECISE, preferred_element_type=F32,
    ) / SEG
    for n, p in order:
        src, mid, dst = pieces(n, p, sizes[n])
        pltpu.make_async_copy(src, mid, in_sem.at[n, p]).wait()
        if n == 3:
            size = sizes[n] // parts
            extra = mean_grad[p * size // SEG:p * size // SEG + 1, :]

            @pl.loop(0, size // GROUP)
            def _(i):
                at = pl.ds(pl.multiple_of(p * size + i * GROUP, GROUP), GROUP)
                rows[at, :] = (rows[at, :].astype(F32) + extra).astype(BF16)

        pltpu.make_async_copy(mid, dst, out_sem.at[n, p]).start()
    segs = means.shape[0]
    for q in range(segs):
        out = None
        for b in range(2):
            part = lax.dot_general(
                source[:, b, :], means[:, b * segs + q, :], (((0,), (0,)), ((), ())),
                precision=PRECISE, preferred_element_type=F32,
            )
            out = part if out is None else out + part
        router_out[:, q * BLOCK:(q + 1) * BLOCK] = out[0:EXPERTS, :]
    for n, p in order:
        _, mid, dst = pieces(n, p, sizes[n])
        pltpu.make_async_copy(mid, dst, out_sem.at[n, p]).wait()


def finish(gate, up, down, direct, source, means, router_t):
    vmem = pl.BlockSpec(memory_space=pltpu.VMEM)
    anywhere = pl.BlockSpec(memory_space=pl.ANY)
    like = [jax.ShapeDtypeStruct(v.shape, v.dtype) for v in (gate, up, down, direct)]
    return pl.pallas_call(
        finish_kernel,
        out_shape=(*like, jax.ShapeDtypeStruct(router_t.shape, F32)),
        in_specs=[anywhere] * 4 + [vmem] * 3,
        out_specs=(anywhere,) * 4 + (vmem,),
        scratch_shapes=[
            pltpu.VMEM((3, *gate.shape), BF16),
            pltpu.VMEM(direct.shape, BF16),
            pltpu.SemaphoreType.DMA((4, 4)),
            pltpu.SemaphoreType.DMA((4, 4)),
        ],
        compiler_params=pltpu.CompilerParams(vmem_limit_bytes=60 * 2**20),
        name="finish",
    )(gate, up, down, direct, source, means, router_t)


def shards(activations, cotangent, router, gate_experts, up_experts, down_experts, route_source):
    router_t = router.T
    gate_t, up_t, down_t, source, means, direct = moved(
        activations, cotangent, gate_experts.transpose(0, 2, 1), up_experts.transpose(0, 2, 1),
        down_experts, router_t, route_source,
    )
    gate_t, up_t, down_t, input_grad, router_grad = finish(
        gate_t, up_t, down_t, direct, source, means, router_t
    )
    return (
        input_grad, gate_t.transpose(0, 2, 1), up_t.transpose(0, 2, 1), down_t, router_grad.T,
    )


def solution(mesh):
    in_specs = (
        P("row", None),
        P("row", None),
        P(),
        P(None, "row", "col"),
        P(None, "row", "col"),
        P(None, "col", "row"),
        P(),
    )
    out_specs = (
        P("row", None),
        P(None, "row", "col"),
        P(None, "row", "col"),
        P(None, "col", "row"),
        P(),
    )
    return jax.shard_map(shards, mesh=mesh, in_specs=in_specs, out_specs=out_specs, check_vma=False)
```

time: 326 us -> 205 us (0.63)
  blocking collectives: 95 us -> 0 us
  local copies, waits for them, and re-layouts: 10.6 us -> 0 us
  Pallas kernels: 211 us -> 204 us
  other arithmetic: 6.53 us -> 0 us
    psum x1 -> x0, blocking collectives: 75.3 us -> none  [shards(): route_grad = lax.psum(partial_value, ('row', 'col'))]
    all_gather x1 -> x0, blocking collectives: 19.7 us -> none  [shards(): all_means = lax.all_gather(own_means, 'row', axis=0, tiled=True)]
    pallas_call x1, Pallas kernels: 211 us -> 196 us  [moved(): pl.pallas_call(kernel, out_shape=(grad, grad, grad, jax.ShapeDtypeStruct(...]
    pallas_call x0 -> x1, Pallas kernels: none -> 8.39 us  [finish(): pl.pallas_call(finish_kernel, out_shape=(*like, jax.ShapeDtypeStruct(rout...]
    unnamed x14 -> x0, local copies, waits for them, and re-layouts: 5.06 us -> none
    mul x5 -> x0, local copies, waits for them, and re-layouts: 4.42 us -> none  [shards(): ordered[:, :, None, :, None] * same[None, None, :, None, :]]
    convert_element_type x3 -> x0, other arithmetic: 3.59 us -> none  [the longest x1 3.58 us: shards(): (direct.astype(F32) + mean_grad[:, None, :] / SEG).reshape(-1, model_width)]
where the time goes in v2:
time: 205 us
  Pallas kernels  204 us (100%)
    pallas_call x1, Pallas kernels, moved(): pl.pallas_call(kernel, out_shape=(grad, grad, grad, jax.ShapeDtypeStruct(...  196 us
    pallas_call x1, Pallas kernels, finish(): pl.pallas_call(finish_kernel, out_shape=(*like, jax.ShapeDtypeStruct(rout...  8.39 us

profile of v2, /device:TPU:1, one launch (start us, length us, event | category | flops | bytes accessed | tf_op | source)
XLA Modules:
  0.0 204.9 jit_solution(13249747969382131038)
XLA Ops:
  0.6 195.8 %experts.1 = (bf16[16,352,128]{2,1,0:T(8,128)(2,1)}, bf16[16,352,128]{2,1,0:T(8,128)(2,1)}, bf16[16,352,128]{2,1,0:T(8,128)(2,1)}, f32[16,8,128]{2,1,0:T(8,128)}...) custom-call(bf16[512,2048]{1,0:T(8,128)(2,1)} %act.1, bf16[512,2048]{1,0:T(8,128)(2,1)} %cot.1, ...), custom_call_target="tpu_custom_call" | custom-call | flops 12000000000 | bytes 16000000 | tf_op jit(solution)/shard_map/experts/pallas_call | solution.py:566
  196.5 8.4 %finish.1 = (bf16[16,352,128]{2,1,0:T(8,128)(2,1)}, bf16[16,352,128]{2,1,0:T(8,128)(2,1)}, bf16[16,352,128]{2,1,0:T(8,128)(2,1)}, bf16[512,2048]{1,0:T(8,128)(2,1)}, f32[16,2048]{1,0:T(8,128)}) custom-call(bf16[16,352,128]{2,1,0:T(8,128)(2,1)} %get-tuple-element.16.gate, bf16[16,352,128]{2,1,0:T(8,128)(2,1)} %get-tuple-element.17.up, ...), custom_call_target="tpu_custom_call" | custom-call | tf_op jit(solution)/shard_map/finish/pallas_call | solution.py:671

commit v3 on v2

--- a/solution.py
+++ b/solution.py
@@ -46,8 +46,8 @@
     experts, tokens, merged, weights, terms, part_out, part_in, deltas,
     direct, from_pair, to_depth, from_depth, depth_sum, to_owner, direct_all, inner,
     spread, spread_t, scores, means, routes, in_row, in_col, source, chooser,
-    e_sem, tok_sem, tok_send, near_sem, near_send, pass_sem, pass_send, m_send, m_recv, p_send, p_recv, d_send, d_recv,
-    t_send, t_recv, s_send, s_recv, z_send, z_recv, o_send, o_recv, a_send, a_recv,
+    e_sem, tok_sem, tok_send, near_sem, near_send, pass_sem, pass_send, m_send, m_recv, p_send, p_recv, d_send, d_recv, d_pass,
+    t_send, t_recv, s_send, s_recv, z_send, z_recv, z_pass, o_send, o_recv, a_send, a_recv, a_pass,
     f_send, f_recv, out_sem, c_send, c_recv, n_send, n_recv, r_send, r_recv, l_send, l_recv,
 ):
     row = lax.axis_index("row")
@@ -292,17 +292,30 @@
         deltas[h, j, 0] = (grad * up * sig * (1.0 + gate * (1.0 - sig))).astype(BF16)
         deltas[h, j, 1] = (grad * gated).astype(BF16)
         deltas[h, j, 2] = (gated * up).astype(BF16)
-        for o in range(1, SIDE):
+        for o in (1, SIDE - 1):
             send(
                 deltas.at[h, j], deltas.at[h, j], d_send.at[h, b], d_recv.at[h, j],
                 (line(h, (own + o) % SIDE), col),
             )
 
+    @pl.loop(0, 4)
+    def _(i):
+        b, h = i // 2, i % 2
+        own = jnp.where(h == 0, x, y)
+        for n, o in ((1, 1), (0, SIDE - 1)):
+            j = SIDE * b + (own + o) % SIDE
+            drain(deltas.at[h, j], d_recv.at[h, j])
+            part = deltas.at[h, j, :, :, pl.ds(n * BLOCK, BLOCK)]
+            send(part, part, d_pass.at[h, b], d_recv.at[h, j], (line(h, (own - o + SIDE) % SIDE), col))
+
     def item(i):
         b, t, h = i // 8, (i // 2) % SIDE, i % 2
         own = jnp.where(h == 0, x, y)
-        q = (own + t) % SIDE
+        q = (own + jnp.where(t < 2, t, 5 - t)) % SIDE
         return b, t, h, q, SIDE * b + q
+
+    def above(o):
+        return (row, (z + o) % DEPTH * 2 + k)
 
     def pair_sum(i):
         b, t, h, q, j = item(i)
@@ -310,13 +323,26 @@
         out = direct[i % 4, k].astype(F32) + from_pair[h, j].astype(F32)
         to_depth[h, j] = out.astype(BF16).reshape(DEPTH, CHUNK, WIDE)
 
-        @pl.loop(1, DEPTH)
-        def _(o):
+        def hop(target, over, slot, sem):
+            to = (z + target) % DEPTH
+            send(to_depth.at[h, j, to], from_depth.at[h, j, slot], z_send.at[h, j], sem.at[h, j], above(over))
+
+        hop(DEPTH - 3, DEPTH - 1, 4, z_pass)
+        hop(3, 1, 5, z_pass)
+        hop(4, DEPTH - 2, 6, z_pass)
+        hop(1, 1, 0, z_recv)
+        hop(DEPTH - 1, DEPTH - 1, 1, z_recv)
+
+    def pass_sum(i):
+        b, t, h, q, j = item(i)
+        drain(from_depth.at[h, j, 4:7], z_pass.at[h, j])
+        for o, slots, into in ((DEPTH - 2, (4, 6), 2), (2, (5,), 3)):
             to = (z + o) % DEPTH
-            send(
-                to_depth.at[h, j, to], from_depth.at[h, j, o - 1], z_send.at[h, j], z_recv.at[h, j],
-                (row, to * 2 + k),
-            )
+            out = to_depth[h, j, to].astype(F32)
+            for slot in slots:
+                out += from_depth[h, j, slot].astype(F32)
+            to_depth[h, j, to] = out.astype(BF16)
+            send(to_depth.at[h, j, to], from_depth.at[h, j, into], z_send.at[h, j], z_recv.at[h, j], above(o))
 
     def send_terms(i):
         b, t, h, q, j = item(i)
@@ -333,7 +359,7 @@
     def backward(i):
         b, t, h, q, j = item(i)
 
-        @pl.when(t > 0)
+        @pl.when(t == SIDE - 1)
         def _():
             drain(deltas.at[h, j], d_recv.at[h, j])
 
@@ -356,24 +382,17 @@
         def _():
             pair_sum(i - 1)
 
-    @pl.loop(0, 8)
-    def _(i):
-        backward(i)
-        send_terms(i)
-
-    @pl.loop(8, 16)
-    def _(i):
-        backward(i)
-
-    pair_sum(15)
+        @pl.when(i > 1)
+        def _():
+            pass_sum(i - 2)
 
     def depth_sums(b):
         @pl.loop(0, 8)
         def _(i):
             _, t, h, q, j = item(b * 8 + i)
-            drain(from_depth.at[h, j], z_recv.at[h, j])
+            drain(from_depth.at[h, j, 0:4], z_recv.at[h, j])
             out = to_depth[h, j, z].astype(F32)
-            for o in range(DEPTH - 1):
+            for o in range(4):
                 out += from_depth[h, j, o].astype(F32)
             depth_sum[h, j] = out.astype(BF16)
             own = jnp.where(h == 0, x, y)
@@ -389,8 +408,9 @@
                     (line(h, q), col),
                 )
 
-    def place(b):
-        return pl.ds(pl.multiple_of(b * SEG + k * (SEG // 2) + z * CHUNK, CHUNK), CHUNK)
+    def place(b, o=0):
+        at = b * SEG + k * (SEG // 2) + (z + o) % DEPTH * CHUNK
+        return direct_all.at[pl.ds(pl.multiple_of(at, CHUNK), CHUNK)]
 
     def half(b):
         return pl.ds(pl.multiple_of(b * SEG + k * (SEG // 2), SEG // 2), SEG // 2)
@@ -404,18 +424,20 @@
                 one = to_owner[0, b, p, :, q * BLOCK:(q + 1) * BLOCK].astype(F32)
                 two = to_owner[1, b, q, :, p * BLOCK:(p + 1) * BLOCK].astype(F32)
                 pieces.append((one + two).astype(BF16))
-        direct_all[place(b), :] = jnp.concatenate(pieces, axis=1)
-
-        @pl.loop(1, DEPTH)
-        def _(o):
-            to = (z + o) % DEPTH
-            send(
-                direct_all.at[place(b)], direct_all.at[place(b)], a_send.at[b], a_recv.at[b],
-                (row, to * 2 + k),
-            )
+        place(b)[...] = jnp.concatenate(pieces, axis=1)
+        for o in (1, DEPTH - 1):
+            send(place(b), place(b), a_send.at[b], a_recv.at[b], above(o))
+        for n, o in enumerate((2, DEPTH - 2)):
+            send(place(b), place(b), a_send.at[b], a_pass.at[b, n], above(o))
+
+    def pass_direct(b):
+        for n, (back, steps) in enumerate(((DEPTH - 2, (1, 2)), (2, (DEPTH - 1,)))):
+            drain(place(b, back), a_pass.at[b, n])
+            for o in steps:
+                send(place(b, back), place(b, back), a_send.at[b], a_recv.at[b], above(o))
 
     def share_direct(b):
-        drain(direct_all.at[0:7 * CHUNK], a_recv.at[b])
+        drain(direct_all.at[0:5 * CHUNK], a_recv.at[b])
         send(direct_all.at[half(b)], direct_all.at[half(b)], f_send.at[b], f_recv.at[b], sibling)
 
     def group(h, g):
@@ -427,7 +449,7 @@
         for h in range(2):
             drain(terms.at[h, b], t_recv.at[h, b])
 
-            @pl.loop(0, HALF // GROUP)
+            @pl.loop(0, HALF // GROUP, unroll=True)
             def _(g):
                 at, chunk = group(h, g)
                 term = terms[h, b, :, pl.ds(at, GROUP), :].reshape(span, LANES)
@@ -437,7 +459,7 @@
         for b in range(2):
             drain(merged.at[h, b, 0:12], m_send.at[h, b])
 
-        @pl.loop(0, HALF // GROUP)
+        @pl.loop(0, HALF // GROUP, unroll=True)
         def _(g):
             at = pl.multiple_of(g * GROUP, GROUP)
             out = None
@@ -453,14 +475,26 @@
                 dst.at[:, pl.ds(h * HALF, HALF), :], out_sem.at[h, n],
             ).start()
 
+    @pl.loop(0, 12)
+    def _(i):
+        backward(i)
+        send_terms(i)
+
     depth_sums(0)
-    pl.loop(8, 12)(send_terms)
+
+    @pl.loop(12, 16)
+    def _(i):
+        backward(i)
+        send_terms(i)
+
+    pair_sum(15)
+    pass_sum(14)
+    pass_sum(15)
     spread_direct(0)
     depth_sums(1)
-    pl.loop(12, 16)(send_terms)
+    products(0)
+    pass_direct(0)
     spread_direct(1)
-    share_direct(0)
-    products(0)
     products(1)
 
     fold = (iota((span, BLOCK), 0) // GROUP == iota((span, BLOCK), 1) % EXPERTS).astype(F32)
@@ -479,8 +513,9 @@
     def _(o):
         send(in_row.at[0], in_row.at[o], r_send, r_recv, ((row + o) % rows_all, col))
 
+    pass_direct(1)
+    share_direct(0)
     gradients(0)
-    share_direct(1)
     drain(in_row.at[1:rows_all], r_recv)
 
     @pl.loop(1, rows_all)
@@ -497,6 +532,7 @@
         send(in_col.at[0], in_col.at[o], l_send, l_recv, (row, (col + o) % cols_all))
 
     gradients(1)
+    share_direct(1)
     for b in range(2):
         drain(direct_all.at[0:SEG // 2], f_recv.at[b])
     copy = pltpu.make_async_copy(direct_all, direct_out, e_sem.at[0])
@@ -525,7 +561,8 @@
 
     for h in range(2):
         for b in range(2):
-            drain(deltas.at[h, 0:3], d_send.at[h, b])
+            drain(deltas.at[h, 0:2], d_send.at[h, b])
+            drain(deltas.at[h, 0], d_pass.at[h, b])
             drain(depth_sum.at[h, 0:3], o_send.at[h, b])
         own = x if h == 0 else y
 
@@ -600,9 +637,9 @@
             pltpu.VMEM((segs, 8, BLOCK), F32),
             pltpu.VMEM((2 * segs, BLOCK), F32),
             dma((3,)), dma((2, 8)), dma, dma((2, 8)), dma((2,)), dma((2, 8)), dma((2,)),
-            dma((2, 2)), dma((2, 8)), dma((2, 8)), dma((2, 2)), dma((2, 2)), dma((2, 8)),
-            dma((2, 8)), dma((2, 2)), dma((4,)), dma((2, 8)), dma((2, 8)), dma((2, 8)),
-            dma((2, 2)), dma((2, 2)), dma((2,)), dma((2,)), dma((2,)), dma((2,)), dma((2, 3)),
+            dma((2, 2)), dma((2, 8)), dma((2, 8)), dma((2, 2)), dma((2, 2)), dma((2, 8)), dma((2, 2)),
+            dma((2, 8)), dma((2, 2)), dma((4,)), dma((2, 8)), dma((2, 8)), dma((2, 8)), dma((2, 8)),
+            dma((2, 2)), dma((2, 2)), dma((2,)), dma((2,)), dma((2, 2)), dma((2,)), dma((2,)), dma((2, 3)),
             dma, dma, dma, dma, dma, dma, dma, dma,
         ],
         compiler_params=pltpu.CompilerParams(

time: 205 us -> 193 us (0.941)
  Pallas kernels: 204 us -> 192 us
    pallas_call x1, Pallas kernels: 196 us -> 183 us  [moved(): pl.pallas_call(kernel, out_shape=(grad, grad, grad, jax.ShapeDtypeStruct(...]
where the time goes in v3:
time: 193 us; the launch traced here: 192 us
  Pallas kernels  192 us (99%)
    pallas_call x1, Pallas kernels, moved(): pl.pallas_call(kernel, out_shape=(grad, grad, grad, jax.ShapeDtypeStruct(...  183 us
    pallas_call x1, Pallas kernels, finish(): pl.pallas_call(finish_kernel, out_shape=(*like, jax.ShapeDtypeStruct(rout...  8.39 us

profile of v3, /device:TPU:1, one launch (start us, length us, event | category | flops | bytes accessed | tf_op | source)
XLA Modules:
  0.0 192.4 jit_solution(18240469269540025164)
XLA Ops:
  0.6 183.4 %experts.1 = (bf16[16,352,128]{2,1,0:T(8,128)(2,1)}, bf16[16,352,128]{2,1,0:T(8,128)(2,1)}, bf16[16,352,128]{2,1,0:T(8,128)(2,1)}, f32[16,8,128]{2,1,0:T(8,128)}...) custom-call(bf16[512,2048]{1,0:T(8,128)(2,1)} %act.1, bf16[512,2048]{1,0:T(8,128)(2,1)} %cot.1, ...), custom_call_target="tpu_custom_call" | custom-call | flops 12000000000 | bytes 16000000 | tf_op jit(solution)/shard_map/experts/pallas_call | solution.py:603
  184.0 8.4 %finish.1 = (bf16[16,352,128]{2,1,0:T(8,128)(2,1)}, bf16[16,352,128]{2,1,0:T(8,128)(2,1)}, bf16[16,352,128]{2,1,0:T(8,128)(2,1)}, bf16[512,2048]{1,0:T(8,128)(2,1)}, f32[16,2048]{1,0:T(8,128)}) custom-call(bf16[16,352,128]{2,1,0:T(8,128)(2,1)} %get-tuple-element.16.gate, bf16[16,352,128]{2,1,0:T(8,128)(2,1)} %get-tuple-element.17.up, ...), custom_call_target="tpu_custom_call" | custom-call | tf_op jit(solution)/shard_map/finish/pallas_call | solution.py:708

commit v4 on v3

--- a/solution.py
+++ b/solution.py
@@ -43,10 +43,10 @@
 def kernel(
     act, cot, gate_t, up_t, down, router_t, wanted,
     gate_out, up_out, down_out, source_out, means_out, direct_out,
-    experts, tokens, merged, weights, terms, part_out, part_in, deltas,
+    experts, tokens, merged, weights, terms, part_out, part_mid, part_in, deltas,
     direct, from_pair, to_depth, from_depth, depth_sum, to_owner, direct_all, inner,
     spread, spread_t, scores, means, routes, in_row, in_col, source, chooser,
-    e_sem, tok_sem, tok_send, near_sem, near_send, pass_sem, pass_send, m_send, m_recv, p_send, p_recv, d_send, d_recv, d_pass,
+    e_sem, tok_sem, tok_send, near_sem, near_send, pass_sem, pass_send, m_send, m_recv, p_send, mid_recv, p_recv, d_send, d_recv, d_pass,
     t_send, t_recv, s_send, s_recv, z_send, z_recv, z_pass, o_send, o_recv, a_send, a_recv, a_pass,
     f_send, f_recv, out_sem, c_send, c_recv, n_send, n_recv, r_send, r_recv, l_send, l_recv,
 ):
@@ -61,6 +61,9 @@
 
     def cross(h, at):
         return jnp.where(h == 0, x * SIDE + at, at * SIDE + y)
+
+    def nth(t):
+        return jnp.where(t == 0, 2, jnp.where(t == 1, 1, jnp.where(t == 2, 3, 0)))
 
     def send(src, dst, send_sem, recv_sem, to):
         pltpu.make_async_remote_copy(
@@ -217,7 +220,7 @@
 
             @pl.loop(0, SIDE)
             def _(t):
-                q = (own + 1 + t) % SIDE
+                q = (own + nth(t)) % SIDE
                 for o in range(SIDE):
                     to = (side + o) % SIDE
                     slot = q * SIDE + to if h == 0 else to * SIDE + q
@@ -247,7 +250,7 @@
         def _(i):
             t, h = i // 2, i % 2
             own = jnp.where(h == 0, x, y)
-            q = (own + 1 + t) % SIDE
+            q = (own + nth(t)) % SIDE
             j = SIDE * b + q
             drain(weights.at[h, j], m_recv.at[h, j])
 
@@ -263,15 +266,31 @@
                 side = tokens[h, j, 0 if n < 2 else 1]
                 part_out[h, j, n] = dot_nt(joined(h, j, n), side).astype(BF16)
 
-            @pl.when(t < SIDE - 1)
+            @pl.when(t == 0)
             def _():
-                send(
-                    part_out.at[h, j], part_in.at[h, b, t], p_send.at[h, j], p_recv.at[h, b],
-                    (line(h, q), col),
-                )
+                for n, o in enumerate((SIDE - 1, 1)):
+                    send(
+                        part_out.at[h, j, :, :, pl.ds(n * BLOCK, BLOCK)], part_mid.at[h, b, n],
+                        p_send.at[h, j], mid_recv.at[h, b, n], (line(h, (own + o) % SIDE), col),
+                    )
 
     forward(0)
     forward(1)
+
+    @pl.loop(0, 4)
+    def _(i):
+        b, h = i // 2, i % 2
+        own = jnp.where(h == 0, x, y)
+        for t, o in enumerate((1, SIDE - 1)):
+            n = 1 - t
+            q = (own + o) % SIDE
+            j = SIDE * b + q
+            lanes = slice(n * BLOCK, (n + 1) * BLOCK)
+            drain(part_mid.at[h, b, n], mid_recv.at[h, b, n])
+            for m in range(3):
+                both = part_out[h, j, m, :, lanes].astype(F32) + part_mid[h, b, n, m].astype(F32)
+                part_out[h, j, m, :, lanes] = both.astype(BF16)
+            send(part_out.at[h, j], part_in.at[h, b, t], p_send.at[h, j], p_recv.at[h, b], (line(h, q), col))
 
     @pl.loop(0, 4)
     def _(i):
@@ -282,7 +301,7 @@
 
         def total(n):
             out = part_out[h, j, n].astype(F32)
-            for o in range(SIDE - 1):
+            for o in range(2):
                 out += part_in[h, b, o, n].astype(F32)
             return out
 
@@ -617,7 +636,8 @@
             pltpu.VMEM((2, 8, SIDE, HALF, LANES), BF16),
             pltpu.VMEM((2, 2, segs, HALF, LANES), BF16),
             pltpu.VMEM((2, 8, 3, HALF, SEG), BF16),
-            pltpu.VMEM((2, 2, 3, 3, HALF, SEG), BF16),
+            pltpu.VMEM((2, 2, 2, 3, HALF, BLOCK), BF16),
+            pltpu.VMEM((2, 2, 2, 3, HALF, SEG), BF16),
             pltpu.VMEM((2, 8, 3, HALF, SEG), BF16),
             pltpu.VMEM((4, 2, SEG // 2, WIDE), BF16),
             pltpu.VMEM((2, 8, SEG // 2, WIDE), BF16),
@@ -637,7 +657,7 @@
             pltpu.VMEM((segs, 8, BLOCK), F32),
             pltpu.VMEM((2 * segs, BLOCK), F32),
             dma((3,)), dma((2, 8)), dma, dma((2, 8)), dma((2,)), dma((2, 8)), dma((2,)),
-            dma((2, 2)), dma((2, 8)), dma((2, 8)), dma((2, 2)), dma((2, 2)), dma((2, 8)), dma((2, 2)),
+            dma((2, 2)), dma((2, 8)), dma((2, 8)), dma((2, 2, 2)), dma((2, 2)), dma((2, 2)), dma((2, 8)), dma((2, 2)),
             dma((2, 8)), dma((2, 2)), dma((4,)), dma((2, 8)), dma((2, 8)), dma((2, 8)), dma((2, 8)),
             dma((2, 2)), dma((2, 2)), dma((2,)), dma((2,)), dma((2, 2)), dma((2,)), dma((2,)), dma((2, 3)),
             dma, dma, dma, dma, dma, dma, dma, dma,
@@ -687,15 +707,15 @@
 
         pltpu.make_async_copy(mid, dst, out_sem.at[n, p]).start()
     segs = means.shape[0]
-    for q in range(segs):
-        out = None
-        for b in range(2):
-            part = lax.dot_general(
-                source[:, b, :], means[:, b * segs + q, :], (((0,), (0,)), ((), ())),
-                precision=PRECISE, preferred_element_type=F32,
-            )
-            out = part if out is None else out + part
-        router_out[:, q * BLOCK:(q + 1) * BLOCK] = out[0:EXPERTS, :]
+    out = None
+    for b in range(2):
+        rows_b = jnp.concatenate([means[:, b * segs + q, :] for q in range(segs)], axis=1)
+        part = lax.dot_general(
+            source[:, b, 0:EXPERTS], rows_b, (((0,), (0,)), ((), ())),
+            precision=PRECISE, preferred_element_type=F32,
+        )
+        out = part if out is None else out + part
+    router_out[...] = out
     for n, p in order:
         _, mid, dst = pieces(n, p, sizes[n])
         pltpu.make_async_copy(mid, dst, out_sem.at[n, p]).wait()

time: 193 us -> 185 us (0.959)
  Pallas kernels: 192 us -> 184 us
    pallas_call x1, Pallas kernels: 183 us -> 177 us  [moved(): pl.pallas_call(kernel, out_shape=(grad, grad, grad, jax.ShapeDtypeStruct(...]
where the time goes in v4:
time: 185 us
  Pallas kernels  184 us (99%)
    pallas_call x1, Pallas kernels, moved(): pl.pallas_call(kernel, out_shape=(grad, grad, grad, jax.ShapeDtypeStruct(...  177 us
    pallas_call x1, Pallas kernels, finish(): pl.pallas_call(finish_kernel, out_shape=(*like, jax.ShapeDtypeStruct(rout...  7.25 us

profile of v4, /device:TPU:1, one launch (start us, length us, event | category | flops | bytes accessed | tf_op | source)
XLA Modules:
  0.0 185.0 jit_solution(10015171015116108674)
XLA Ops:
  0.6 177.1 %experts.1 = (bf16[16,352,128]{2,1,0:T(8,128)(2,1)}, bf16[16,352,128]{2,1,0:T(8,128)(2,1)}, bf16[16,352,128]{2,1,0:T(8,128)(2,1)}, f32[16,8,128]{2,1,0:T(8,128)}...) custom-call(bf16[512,2048]{1,0:T(8,128)(2,1)} %act.1, bf16[512,2048]{1,0:T(8,128)(2,1)} %cot.1, ...), custom_call_target="tpu_custom_call" | custom-call | flops 12000000000 | bytes 16000000 | tf_op jit(solution)/shard_map/experts/pallas_call | solution.py:622
  177.7 7.3 %finish.1 = (bf16[16,352,128]{2,1,0:T(8,128)(2,1)}, bf16[16,352,128]{2,1,0:T(8,128)(2,1)}, bf16[16,352,128]{2,1,0:T(8,128)(2,1)}, bf16[512,2048]{1,0:T(8,128)(2,1)}, f32[16,2048]{1,0:T(8,128)}) custom-call(bf16[16,352,128]{2,1,0:T(8,128)(2,1)} %get-tuple-element.16.gate, bf16[16,352,128]{2,1,0:T(8,128)(2,1)} %get-tuple-element.17.up, ...), custom_call_target="tpu_custom_call" | custom-call | tf_op jit(solution)/shard_map/finish/pallas_call | solution.py:728

commit v5 on v4

--- a/solution.py
+++ b/solution.py
@@ -189,7 +189,7 @@
         own = x if h == 0 else y
         return [SIDE * b + (own + o) % SIDE for o in range(1, SIDE)]
 
-    for b in range(2):
+    def pass_tokens(b):
         for o in range(SIDE - 1):
             for h in range(2):
                 j = others(b, h)[o]
@@ -202,10 +202,14 @@
                     one = tokens.at[h, j, n, piece]
                     to = (row, (z + step) % DEPTH * 2 + k)
                     send(one, one, near_send.at[1], near_sem.at[h, j], to)
+
     for load in loads:
         load.wait()
 
     for b in range(2):
+        if b == 1:
+            pass_tokens(0)
+            pass_tokens(1)
         for h in range(2):
 
             @pl.loop(0, HALF // GROUP)

time: 185 us -> 183 us (0.989)
  Pallas kernels: 184 us -> 182 us
    pallas_call x1, Pallas kernels: 177 us -> 175 us  [moved(): pl.pallas_call(kernel, out_shape=(grad, grad, grad, jax.ShapeDtypeStruct(...]
where the time goes in v5:
time: 183 us; the launch traced here: 182 us
  Pallas kernels  182 us (99%)
    pallas_call x1, Pallas kernels, moved(): pl.pallas_call(kernel, out_shape=(grad, grad, grad, jax.ShapeDtypeStruct(...  175 us
    pallas_call x1, Pallas kernels, finish(): pl.pallas_call(finish_kernel, out_shape=(*like, jax.ShapeDtypeStruct(rout...  7.25 us

profile of v5, /device:TPU:1, one launch (start us, length us, event | category | flops | bytes accessed | tf_op | source)
XLA Modules:
  0.0 182.5 jit_solution(1038173549183001383)
XLA Ops:
  0.6 174.6 %experts.1 = (bf16[16,352,128]{2,1,0:T(8,128)(2,1)}, bf16[16,352,128]{2,1,0:T(8,128)(2,1)}, bf16[16,352,128]{2,1,0:T(8,128)(2,1)}, f32[16,8,128]{2,1,0:T(8,128)}...) custom-call(bf16[512,2048]{1,0:T(8,128)(2,1)} %act.1, bf16[512,2048]{1,0:T(8,128)(2,1)} %cot.1, ...), custom_call_target="tpu_custom_call" | custom-call | flops 12000000000 | bytes 16000000 | tf_op jit(solution)/shard_map/experts/pallas_call | solution.py:626
  175.2 7.3 %finish.1 = (bf16[16,352,128]{2,1,0:T(8,128)(2,1)}, bf16[16,352,128]{2,1,0:T(8,128)(2,1)}, bf16[16,352,128]{2,1,0:T(8,128)(2,1)}, bf16[512,2048]{1,0:T(8,128)(2,1)}, f32[16,2048]{1,0:T(8,128)}) custom-call(bf16[16,352,128]{2,1,0:T(8,128)(2,1)} %get-tuple-element.16.gate, bf16[16,352,128]{2,1,0:T(8,128)(2,1)} %get-tuple-element.17.up, ...), custom_call_target="tpu_custom_call" | custom-call | tf_op jit(solution)/shard_map/finish/pallas_call | solution.py:732
